TPU v7x, 512 devices: a whole 4x8x8 slice. The times are simulated.
512 devices in a mesh: fsdp: 64 (over y_lo, z, x), tp: 8 (over y_hi, core).
Axes of the slice: x: 4, y: 8 (y_hi: 4, y_lo: 2; y = y_hi * 2 + y_lo), z: 8, core: 2. Of those that a mesh axis runs over, the one named last changes fastest.
Arguments:
- hidden: bfloat16 [4096, 5120], P('fsdp', 'tp'), may hold values from -6 to 6
- next_hidden: bfloat16 [4096, 5120], P('fsdp', 'tp'), may hold values from -6 to 6
- gain: bfloat16 [5120], replicated, may hold values from 0.5 to 2
- w_query: bfloat16 [5120, 4096], P('fsdp', 'tp'), may hold values from -0.078125 to 0.078125
- w_key: bfloat16 [5120, 1024], P('fsdp', 'tp'), may hold values from -0.078125 to 0.078125
- w_value: bfloat16 [5120, 1024], P('fsdp', 'tp'), may hold values from -0.078125 to 0.078125
- w_out: bfloat16 [4096, 5120], P('tp', 'fsdp'), may hold values from -0.09375 to 0.09375
- key_cache: bfloat16 [4096, 8, 128, 128], P('fsdp', 'tp'), may hold values from -400 to 400
- value_cache: bfloat16 [4096, 8, 128, 128], P('fsdp', 'tp'), may hold values from -6 to 6
- lengths: int32 [4096], P('fsdp'), may hold values from 1 to 128, as said below
- positions: int32 [4096], P('fsdp'), may hold values from 1 to 8319, as said below
Outputs:
- layer_out: bfloat16 [64, 2, 64, 5120], P(None, None, 'fsdp', 'tp')
Inputs may be any that keep to these rules, and one draw needn't show every extreme that they name: `lengths`: the first sequence of every rollout group has all 128 slots live, the second exactly one. positions[r] >= lengths[r]; the new tokens of sequence r stand at positions[r] and positions[r] + 1.
All inputs are finite; a program needn't handle non-finite values.
Results may differ from a plain program's by a relative error of at most 0.012.
Values may be sent and summed in bfloat16 or wider, within the bound.
A program may use at most 128 MiB of HBM per device.

v0:
```python
import jax
import jax.numpy as jnp
from jax import lax
from jax.sharding import PartitionSpec as P

RMS_EPS = 1e-06
ROPE_BASE = 1000000.0


def normalize(rows_in, gain):
    values = rows_in.astype(jnp.float32)
    square = jnp.mean(values * values, axis=-1, keepdims=True)
    return (values * lax.rsqrt(square + RMS_EPS) * gain.astype(jnp.float32)).astype(jnp.bfloat16)


def rotate(vectors, where_at):
    half = vectors.shape[-1] // 2
    freqs = ROPE_BASE ** (-(2.0 * jnp.arange(half, dtype=jnp.float32)) / vectors.shape[-1])
    angle = where_at.astype(jnp.float32)[:, :, None, None] * freqs
    cosine = jnp.cos(angle)
    sine = jnp.sin(angle)
    first = vectors[..., :half]
    second = vectors[..., half:]
    return jnp.concatenate(
        [first * cosine - second * sine, second * cosine + first * sine], axis=-1
    )


def attend(queries, keys_new, values_new, key_cache, value_cache, lengths):
    score_scale = queries.shape[-1] ** (-0.5)
    cache_scores = (
        jnp.einsum("srkgd,rkcd->srkgc", queries, key_cache, preferred_element_type=jnp.float32)
        * score_scale
    )
    live = jnp.arange(key_cache.shape[2], dtype=jnp.int32)[None, :] < lengths[:, None]
    cache_scores = jnp.where(live[None, :, None, None, :], cache_scores, -jnp.inf)
    new_scores = (
        jnp.einsum("srkgd,trkd->srkgt", queries, keys_new, preferred_element_type=jnp.float32)
        * score_scale
    )
    causal = jnp.arange(2, dtype=jnp.int32)[:, None] >= jnp.arange(2, dtype=jnp.int32)[None, :]
    new_scores = jnp.where(causal[:, None, None, None, :], new_scores, -jnp.inf)
    row_top = jnp.maximum(jnp.max(cache_scores, axis=-1), jnp.max(new_scores, axis=-1))[..., None]
    cache_probs = jnp.exp(cache_scores - row_top)
    new_probs = jnp.exp(new_scores - row_top)
    total = jnp.sum(cache_probs, axis=-1) + jnp.sum(new_probs, axis=-1)
    cache_weights = cache_probs.astype(jnp.bfloat16)
    new_weights = new_probs.astype(jnp.bfloat16)
    mixed = jnp.einsum(
        "srkgc,rkcd->srkgd", cache_weights, value_cache, preferred_element_type=jnp.float32
    )
    mixed = mixed + jnp.einsum(
        "srkgt,trkd->srkgd", new_weights, values_new, preferred_element_type=jnp.float32
    )
    return (mixed / total[..., None]).astype(jnp.bfloat16)


def on_device(
    hidden,
    next_hidden,
    gain,
    w_query,
    w_key,
    w_value,
    w_out,
    key_cache,
    value_cache,
    lengths,
    positions,
):
    row_count = hidden.shape[0]
    width_local = hidden.shape[1]
    full_rows = (
        lax.all_gather(hidden, "tp", axis=1, tiled=True),
        lax.all_gather(next_hidden, "tp", axis=1, tiled=True),
    )
    both = jnp.stack([full_rows[0], full_rows[1]])
    normed = normalize(both, gain).reshape(2 * row_count, both.shape[2])
    wide_query, wide_key, wide_value, wide_out = (
        lax.all_gather(w_query, "fsdp", axis=0, tiled=True),
        lax.all_gather(w_key, "fsdp", axis=0, tiled=True),
        lax.all_gather(w_value, "fsdp", axis=0, tiled=True),
        lax.all_gather(w_out, "fsdp", axis=1, tiled=True),
    )
    queries = jnp.dot(normed, wide_query, preferred_element_type=jnp.float32)
    keys_new = jnp.dot(normed, wide_key, preferred_element_type=jnp.float32)
    values_new = jnp.dot(normed, wide_value, preferred_element_type=jnp.float32)
    head_size = key_cache.shape[3]
    kv_local = key_cache.shape[1]
    query_local = queries.shape[1] // head_size
    where_at = positions[None, :] + jnp.arange(2, dtype=jnp.int32)[:, None]
    queries = rotate(queries.reshape(2, row_count, query_local, head_size), where_at).astype(
        jnp.bfloat16
    )
    keys_new = rotate(keys_new.reshape(2, row_count, kv_local, head_size), where_at).astype(
        jnp.bfloat16
    )
    values_new = values_new.reshape(2, row_count, kv_local, head_size).astype(jnp.bfloat16)
    grouped = queries.reshape(2, row_count, kv_local, query_local // kv_local, head_size)
    attended = attend(grouped, keys_new, values_new, key_cache, value_cache, lengths)
    attended = attended.reshape(2 * row_count, query_local * head_size)
    projected = jnp.dot(attended, wide_out, preferred_element_type=jnp.float32)
    summed = lax.psum(projected, "tp")
    mine = lax.dynamic_slice_in_dim(summed, lax.axis_index("tp") * width_local, width_local, 1)
    local_rows = jnp.stack([hidden, next_hidden]).astype(jnp.float32)
    layer = (local_rows + mine.reshape(2, row_count, width_local)).astype(jnp.bfloat16)
    return lax.all_to_all(layer[None], "fsdp", split_axis=2, concat_axis=0, tiled=True)


def solution(mesh):
    placed = (
        P("fsdp", "tp"),
        P("fsdp", "tp"),
        P(),
        P("fsdp", "tp"),
        P("fsdp", "tp"),
        P("fsdp", "tp"),
        P("tp", "fsdp"),
        P("fsdp", "tp", None, None),
        P("fsdp", "tp", None, None),
        P("fsdp"),
        P("fsdp"),
    )
    return jax.shard_map(
        on_device,
        mesh=mesh,
        in_specs=placed,
        out_specs=P(None, None, "fsdp", "tp"),
        check_vma=False,
    )
```

profile of v0, /device:TPU:1, one launch (start us, length us, event | category | flops | bytes accessed | tf_op | source)
XLA Modules:
  0.0 1362.3 jit_solution(13352651455126779951)
XLA Ops:
  6.5 0.0 copy-start
  6.5 0.0 copy-start.7
  6.5 0.0 copy-start.5
  6.5 0.0 all-gather.7.cloned.1.call-start
  6.5 0.7 all-gather.7.cloned.1.call-update
  7.3 0.0 all-gather.9.cloned.1.call-start
  7.3 0.7 all-gather.9.cloned.1.call-update
  8.0 0.0 all-gather.5.cloned.1.call-start
  8.1 0.7 all-gather.5.cloned.1.call-update
  8.7 0.0 all-gather.11.cloned.1.call-start
  8.8 0.5 all-gather.11.cloned.1.call-update
  9.3 0.0 all-reduce.2.cloned.1.call-start
  9.4 1.3 convert_element_type.78
  10.7 22.1 %all_gather.18 = bf16[64,5120]{1,0:T(8,128)(2,1)S(1)} all-gather(bf16[64,640]{1,0:T(8,128)(2,1)} %param.11), channel_id=1, replica_groups=mesh['fsdp'=64,'tp'=8] {'tp'}, dimensions={1}, use_global_device_ids=true | all-gather | bytes 737280 | tf_op jit(solution)/shard_map/all_gather | solution.py:74
  32.8 15.4 %all_gather.19 = bf16[64,5120]{1,0:T(8,128)(2,1)S(1)} all-gather(bf16[64,640]{1,0:T(8,128)(2,1)} %param.12), channel_id=1, replica_groups=mesh['fsdp'=64,'tp'=8] {'tp'}, dimensions={1}, use_global_device_ids=true | all-gather | bytes 737280 | tf_op jit(solution)/shard_map/all_gather | solution.py:75
  48.2 0.4 fusion
  48.6 0.5 iota_compare_fusion.1
  49.1 0.0 copy-done.7
  49.1 0.5 add_rsqrt_fusion
  49.6 0.0 copy-done.5
  49.6 0.1 iota_compare_fusion
  49.7 0.3 multiply_cosine_fusion.1
  50.0 222.7 %all-gather.7.cloned.1.call-done = bf16[5120,128]{1,0:T(8,128)(2,1)} async-done(((bf16[80,128]{1,0:T(8,128)(2,1)}), bf16[5120,128]{1,0:T(8,128)(2,1)}) %all-gather.7.cloned.1.call-update) | async-done | bytes 1310736 | tf_op jit(solution)/shard_map/all_gather | solution.py:81
  272.6 1.9 fusion.29
  274.6 0.3 fusion.76
  274.9 0.7 maximum_bitcast_fusion
  275.6 297.2 %all-gather.9.cloned.1.call-done = bf16[5120,128]{1,0:T(8,128)(2,1)} async-done(((bf16[80,128]{1,0:T(8,128)(2,1)}), bf16[5120,128]{1,0:T(8,128)(2,1)}) %all-gather.9.cloned.1.call-update) | async-done | bytes 1310736 | tf_op jit(solution)/shard_map/all_gather | solution.py:82
  572.8 2.5 fusion.35
  575.3 309.7 %all-gather.5.cloned.1.call-done = bf16[5120,512]{1,0:T(8,128)(2,1)} async-done(((bf16[80,512]{1,0:T(8,128)(2,1)}), bf16[5120,512]{1,0:T(8,128)(2,1)}) %all-gather.5.cloned.1.call-update) | async-done | bytes 5242896 | tf_op jit(solution)/shard_map/all_gather | solution.py:80
  885.0 0.0 copy-start.4
  885.0 7.9 copy.22
  892.9 0.0 copy-done.4
  892.9 0.0 copy-start.3
  892.9 0.0 copy-start.9
  892.9 4.4 fusion.7
  897.3 0.2 subtract_convert_fusion
  897.5 0.0 copy-start.8
  897.5 0.1 pad_maximum_fusion.1
  897.6 0.0 copy-done.3
  897.6 0.0 copy-done.9
  897.6 0.0 copy-start.6
  897.6 1.3 fusion.82
  898.9 0.0 copy-done
  899.0 1.3 fusion.81
  900.3 0.3 fusion.65
  900.6 0.4 fusion.51
  901.1 0.0 copy-done.8
  901.1 0.3 fusion.72
  901.4 0.0 copy-done.6
  901.4 0.7 fusion.47
  902.1 0.1 copy.27
  902.2 291.8 %all-gather.11.cloned.1.call-done = bf16[512,5120]{0,1:T(8,128)(2,1)} async-done(((bf16[512,80]{0,1:T(8,128)(2,1)}), bf16[512,5120]{0,1:T(8,128)(2,1)}) %all-gather.11.cloned.1.call-update) | async-done | bytes 5242896 | tf_op jit(solution)/shard_map/all_gather | solution.py:83
  1194.0 5.8 fusion.55
  1199.7 0.0 copy-start.1
  1199.7 0.0 copy-start.2
  1199.7 0.0 all-reduce.2.cloned.1.call-update
  1199.8 134.2 %all-reduce.2.cloned.1.call-done = f32[128,5120]{1,0:T(8,128)} async-done(((f32[128,5120]{1,0:T(8,128)}), f32[128,5120]{1,0:T(8,128)}) %all-reduce.2.cloned.1.call-update) | async-done | bytes 2621456 | tf_op jit(solution)/shard_map/psum | solution.py:103
  1333.9 1.0 constant_dynamic-slice_fusion
  1334.9 0.0 copy-done.1
  1334.9 0.0 copy-done.2
  1335.0 0.2 copy.28
  1335.2 20.0 %all_to_all.18 = bf16[1,2,64,640]{3,1,0,2:T(2,128)(2,1)S(1)} all-to-all(bf16[1,2,64,640]{3,1,0,2:T(2,128)(2,1)S(1)} %copy.28), channel_id=1, replica_groups=mesh['fsdp'=64,'tp'=8] {'fsdp'}, dimensions={2} | all-to-all | bytes 327680 | tf_op jit(solution)/shard_map/all_to_all | solution.py:107
  1355.2 0.7 copy.60
  (5 shorter events, 0.1 us)
Async XLA Ops:
  6.5 892.4 %copy-start = (bf16[64,1,128,128]{3,2,1,0:T(8,128)(2,1)S(1)}, bf16[64,1,128,128]{3,2,1,0:T(8,128)(2,1)}, u32[]{:S(2)}) copy-start(bf16[64,1,128,128]{3,2,1,0:T(8,128)(2,1)} %param.18) | copy-start | bytes 6291460
  6.5 42.5 %copy-start.7 = (s32[64]{0:T(128)S(1)}, s32[64]{0:T(128)}, u32[]{:S(2)}) copy-start(s32[64]{0:T(128)} %param.21) | copy-start | bytes 772
  6.5 43.1 %copy-start.5 = (s32[64]{0:T(128)S(1)}, s32[64]{0:T(128)}, u32[]{:S(2)}) copy-start(s32[64]{0:T(128)} %param.20) | copy-start | bytes 772
  6.5 266.1 %all-gather.7.cloned.1.call-start = ((), (), s32[]{:S(2)}) async-start(), calls=%async_computation.2 | async-start | bytes 1331200 | tf_op jit(solution)/shard_map/all_gather | solution.py:81
  7.3 565.5 %all-gather.9.cloned.1.call-start = ((), (), s32[]{:S(2)}) async-start(), calls=%async_computation.3 | async-start | bytes 1331200 | tf_op jit(solution)/shard_map/all_gather | solution.py:82
  8.0 877.0 %all-gather.5.cloned.1.call-start = ((), (), s32[]{:S(2)}) async-start(), calls=%async_computation.1 | async-start | bytes 5324800 | tf_op jit(solution)/shard_map/all_gather | solution.py:80
  8.7 1185.2 %all-gather.11.cloned.1.call-start = ((), (), s32[]{:S(2)}) async-start(), calls=%async_computation.4 | async-start | bytes 5324800 | tf_op jit(solution)/shard_map/all_gather | solution.py:83
  9.3 1324.6 %all-reduce.2.cloned.1.call-start = ((), (), s32[]{:S(2)}) async-start(), calls=%async_computation.5 | async-start | bytes 5242880 | tf_op jit(solution)/shard_map/psum | solution.py:103
  885.0 7.9 copy-start.4
  892.9 4.7 copy-start.3
  892.9 4.7 copy-start.9
  897.5 3.6 copy-start.8
  897.6 3.8 copy-start.6
  1199.7 135.2 %copy-start.1 = (bf16[64,640]{1,0:T(8,128)(2,1)S(1)}, bf16[64,640]{1,0:T(8,128)(2,1)}, u32[]{:S(2)}) copy-start(bf16[64,640]{1,0:T(8,128)(2,1)} %param.12) | copy-start | bytes 245764
  1199.7 135.2 %copy-start.2 = (bf16[64,640]{1,0:T(8,128)(2,1)S(1)}, bf16[64,640]{1,0:T(8,128)(2,1)}, u32[]{:S(2)}) copy-start(bf16[64,640]{1,0:T(8,128)(2,1)} %param.11) | copy-start | bytes 245764
Sparse Core Ops, SparseCore 0:
  9.4 263.1 all-gather.6
  274.7 298.0 all-gather.8
  574.9 310.0 all-gather.4
  887.0 306.9 all-gather.10
  1199.9 134.0 all-reduce.1
where the time goes:
time: 1360 us
  waiting for transfers between devices  1260 us (93%)
  blocking collectives  57.5 us (4%)
  matrix products  18.3 us (1%)
    all_gather x1, waiting for transfers between devices, on_device(): lax.all_gather(w_query, 'fsdp', axis=0, tiled=True)  310 us
    all_gather x1, waiting for transfers between devices, on_device(): lax.all_gather(w_value, 'fsdp', axis=0, tiled=True)  297 us
    all_gather x1, waiting for transfers between devices, on_device(): lax.all_gather(w_out, 'fsdp', axis=1, tiled=True)  292 us
    all_gather x1, waiting for transfers between devices, on_device(): lax.all_gather(w_key, 'fsdp', axis=0, tiled=True)  223 us
    psum x1, waiting for transfers between devices, on_device(): summed = lax.psum(projected, 'tp')  134 us
  transfers between devices with their start and end apart: 5, of which 5 were waited for; matrix products, arithmetic and copies ran while one was open for 2% of the time, Pallas kernels for 0%

commit v1 on v0

v1 whole, which is shorter than its diff:
```python
import functools

import jax
import jax.numpy as jnp
from jax import lax
from jax.experimental import pallas as pl
from jax.experimental.pallas import tpu as pltpu
from jax.sharding import PartitionSpec as P

RMS_EPS = 1e-06
ROPE_BASE = 1000000.0
MESH = pl.DeviceIdType.MESH
NX, NZ, NYH = 4, 8, 4
CHUNK = 16

f32, bf16 = jnp.float32, jnp.bfloat16


def one_hot_rows(out_dims, source_of):
    count = 1
    for size in out_dims:
        count *= size
    row = lax.broadcasted_iota(jnp.int32, (count, count), 0)
    column = lax.broadcasted_iota(jnp.int32, (count, count), 1)
    digits, shift = [], 0
    for size in reversed(out_dims):
        bits = size.bit_length() - 1
        digits.append(lax.shift_right_logical(row, shift) & (size - 1))
        shift += bits
    digits.reverse()
    return jnp.where(source_of(*digits) == column, 1.0, 0.0).astype(bf16)


def pick(matrix, rows):
    return jnp.dot(matrix, rows, preferred_element_type=f32)


def layer_kernel(
    hid, nxt, gain, wq, wk, wv, wot, cos_ref, sin_ref, live_ref, kc_hbm, vc_hbm,
    out,
    wa, wb, oa, ob, xs, xg, xn, ssb, ssr, qs, qr, kc, vc, q3, att3, attb,
    ps, pr, pk, sp, rb, rr, zs, zr, xo, xr,
    cache_sem, xs_send, xs_recv, sib_send, sib_recv, res_send, res_recv,
    ax_send, ax_recv, az_send, az_recv, bx_send, bx_recv, bz_send, bz_recv,
    pair_send, pair_recv, core_send, core_recv, y_send, y_recv,
    za_send, za_recv, xa_send, xa_recv,
):
    rows = hid.shape[0]
    half = rows // 2
    both = 2 * rows
    width = hid.shape[1]
    block = wq.shape[0]
    tile_blocks = NYH
    f, t = lax.axis_index("fsdp"), lax.axis_index("tp")
    x, z, yl = lax.rem(f, NX), lax.rem(f // NX, NZ), f // (NX * NZ)
    yh, c = t // 2, lax.rem(t, 2)

    def dev(x_, z_, yl_, yh_, c_):
        return ((yl_ * NZ + z_) * NX + x_, yh_ * 2 + c_)

    def remote(src, dst, send, recv, where):
        return pltpu.make_async_remote_copy(
            src_ref=src, dst_ref=dst, send_sem=send, recv_sem=recv,
            device_id=where, device_id_type=MESH,
        )

    def arrived(dst, sem):
        pltpu.make_async_copy(dst, dst, sem).wait()

    sent = []

    def send(*args):
        copy = remote(*args)
        copy.start()
        sent.append(copy)

    key_load = pltpu.make_async_copy(kc_hbm, kc, cache_sem.at[0])
    value_load = pltpu.make_async_copy(vc_hbm, vc, cache_sem.at[1])
    key_load.start()
    value_load.start()

    y = 2 * yh + yl
    ny = 2 * NYH
    sib = dev(x, z, yl, yh, 1 - c)
    partner = dev(x, z, 1 - yl, yh, c)
    places = [dev(lax.rem(x + d, NX), z, yl, yh, c) for d in range(1, NX)]
    places += [dev(x, lax.rem(z + d, NZ), yl, yh, c) for d in range(1, NZ)]
    for d in range(1, ny):
        yy = lax.rem(y + d, ny)
        places.append(dev(x, z, lax.rem(yy, 2), yy // 2, c))
    places.append(sib)
    barrier = pltpu.get_barrier_semaphore()
    for where in places:
        pl.semaphore_signal(barrier, inc=1, device_id=where, device_id_type=MESH)

    mine = pl.ds(pl.multiple_of(x * block, block), block)
    cut = wa.shape[2]
    own = jnp.concatenate([wq[...], wk[...], wv[...]], axis=1)
    wa[z, mine, :] = own[:, :cut]
    wb[z, mine, :] = own[:, cut:]
    ocut = oa.shape[2]
    oa[z, mine, :] = wot[:, :ocut]
    ob[z, mine, :] = wot[:, ocut:]
    xs[0:rows, :] = hid[...]
    xs[rows:both, :] = nxt[...]
    pl.semaphore_wait(barrier, len(places))

    yl_to = yh // (NYH // 2)
    tile_me = lax.rem(yh, NYH // 2) * 2 + c
    src_me = yl * (NYH // 2) + lax.rem(yh, NYH // 2)
    for k in range(NYH):
        is_self = jnp.logical_and(yl_to == yl, yh == k)
        there = dev(x, z, yl_to, k, c)
        away = remote(xs, xg.at[yl, tile_me], xs_send.at[k], xs_recv.at[src_me], there)
        here = pltpu.make_async_copy(xs, xg.at[yl, tile_me], xs_recv.at[src_me])
        pl.when(jnp.logical_not(is_self))(away.start)
        pl.when(is_self)(here.start)

    up = dev(x, lax.rem(z + 1, NZ), yl, yh, c)
    down = dev(x, lax.rem(z + NZ - 1, NZ), yl, yh, c)
    last = NZ // 2 - 1

    def first_x(buf, s):
        for d in range(1, NX):
            there = dev(lax.rem(x + d, NX), z, yl, yh, c)
            send(buf.at[z, mine], buf.at[z, mine], ax_send.at[s, d - 1], ax_recv.at[s, d - 1], there)

    def wait_first_x(buf, s):
        for d in range(1, NX):
            xx = lax.rem(x + NX - d, NX)
            arrived(buf.at[z, pl.ds(pl.multiple_of(xx * block, block), block)], ax_recv.at[s, d - 1])

    def slab_parts(k):
        if k == last:
            h = NX * block // 2
            return pl.ds(0, h), pl.ds(h, h)
        return pl.ds(0, NX * block), pl.ds(0, NX * block)

    def a_send(buf, s, k):
        p_up, p_down = slab_parts(k)
        zz = lax.rem(z + NZ - k, NZ)
        send(buf.at[zz, p_up], buf.at[zz, p_up], az_send.at[s, 0, k], az_recv.at[s, 0, k], up)
        zz = lax.rem(z + k, NZ)
        send(buf.at[zz, p_down], buf.at[zz, p_down], az_send.at[s, 1, k], az_recv.at[s, 1, k], down)

    def a_wait(buf, s, k):
        p_up, p_down = slab_parts(k)
        arrived(buf.at[lax.rem(z + NZ - 1 - k, NZ), p_up], az_recv.at[s, 0, k])
        arrived(buf.at[lax.rem(z + 1 + k, NZ), p_down], az_recv.at[s, 1, k])

    def b_send(buf, s, k):
        zz = lax.rem(z + NZ - k, NZ)
        send(buf.at[zz, mine], buf.at[zz, mine], bz_send.at[s, 0, k], bz_recv.at[s, 0, k], up)
        if k < last:
            zz = lax.rem(z + k, NZ)
            send(buf.at[zz, mine], buf.at[zz, mine], bz_send.at[s, 1, k], bz_recv.at[s, 1, k], down)

    def b_wait(buf, s, k):
        arrived(buf.at[lax.rem(z + NZ - 1 - k, NZ), mine], bz_recv.at[s, 0, k])
        if k < last:
            arrived(buf.at[lax.rem(z + 1 + k, NZ), mine], bz_recv.at[s, 1, k])

    def b_spread(buf, s, offsets):
        for o in offsets:
            zz = lax.rem(z + NZ + o, NZ)
            for d in range(1, NX):
                there = dev(lax.rem(x + d, NX), z, yl, yh, c)
                remote(buf.at[zz, mine], buf.at[zz, mine],
                       bx_send.at[s, d - 1], bx_recv.at[s, d - 1], there).start()

    def spread_after(k):
        return (-1 - k,) if k == last else (-1 - k, 1 + k)

    def wait_spread(buf, s):
        for d in range(1, NX):
            xx = lax.rem(x + NX - d, NX)
            arrived(buf.at[:, pl.ds(pl.multiple_of(xx * block, block), block)], bx_recv.at[s, d - 1])

    first_x(wa, 0)
    b_send(wb, 0, 0)
    b_spread(wb, 0, (0,))

    away_rows = half * (1 - yl)
    own_rows = half * yl
    for s in range(2):
        src = xs.at[pl.ds(pl.multiple_of(s * rows + away_rows, half), half)]
        send(src, rr.at[yl, pl.ds(s * half, half)], res_send.at[s], res_recv.at[s], partner)
        rr[yl, s * half:(s + 1) * half, :] = xs[pl.ds(pl.multiple_of(s * rows + own_rows, half), half), :]

    wait_first_x(wa, 0)
    a_send(wa, 0, 0)
    first_x(oa, 1)
    b_send(ob, 1, 0)
    for k in range(last):
        b_wait(wb, 0, k)
        b_send(wb, 0, k + 1)
        b_spread(wb, 0, spread_after(k))
        a_wait(wa, 0, k)
        a_send(wa, 0, k + 1)

    for k in range(NYH):
        slot = xg.at[k // (NYH // 2), (k % (NYH // 2)) * 2 + c]
        arrived(slot, xs_recv.at[k])
        send(slot, slot, sib_send.at[k], sib_recv.at[k], sib)
    b_wait(wb, 0, last)
    b_spread(wb, 0, spread_after(last))
    for k in range(NYH):
        arrived(xg.at[k // (NYH // 2), (k % (NYH // 2)) * 2 + (1 - c)], sib_recv.at[k])

    for g in range(2):
        total = jnp.zeros((both, 1), f32)
        for j in range(tile_blocks):
            values = xg[g, j].astype(f32)
            total = total + jnp.sum(values * values, axis=1, keepdims=True)
            xn[g, :, j * width:(j + 1) * width] = (values * gain[yl * tile_blocks + j]).astype(bf16)
        ssb[g] = jnp.broadcast_to(total, (both, 128))
    send(ssb.at[1 - yl], ssr, pair_send.at[0], pair_recv.at[0], partner)

    for s in range(2):
        arrived(rr.at[1 - yl, pl.ds(s * half, half)], res_recv.at[s])
    order = one_hot_rows((NZ, 2, NX), lambda z_, s_, x_: s_ * half + z_ * NX + x_)
    for g in range(2):
        rr[g] = pick(order, rr[g]).astype(bf16)

    a_wait(wa, 0, last)
    wait_spread(wb, 0)
    wait_first_x(oa, 1)
    a_send(oa, 1, 0)
    b_spread(ob, 1, (0,))
    b_wait(ob, 1, 0)
    b_send(ob, 1, 1)
    b_spread(ob, 1, spread_after(0))
    depth = NZ * NX * block
    weight_a = wa[...].reshape(depth, cut)
    weight_b = wb[...].reshape(depth, wb.shape[2])
    theirs = xn[1 - yl]
    qs[:, :cut] = jnp.dot(theirs, weight_a, preferred_element_type=f32).astype(bf16)
    qs[:, cut:] = jnp.dot(theirs, weight_b, preferred_element_type=f32).astype(bf16)
    send(qs, qr, pair_send.at[1], pair_recv.at[1], partner)
    ours = xn[yl]
    got_a = jnp.dot(ours, weight_a, preferred_element_type=f32)
    got_b = jnp.dot(ours, weight_b, preferred_element_type=f32)
    got = jnp.concatenate([got_a, got_b], axis=1)

    def out_step(k):
        a_wait(oa, 1, k)
        a_send(oa, 1, k + 1)
        b_wait(ob, 1, k + 1)
        if k + 1 < last:
            b_send(ob, 1, k + 2)
        b_spread(ob, 1, spread_after(k + 1))

    if last > 0:
        out_step(0)
    arrived(ssr, pair_recv.at[0])
    square = (ssb[yl] + ssr[...]) * (1.0 / (2 * tile_blocks * width))
    inverse = lax.rsqrt(square[:, :1] + RMS_EPS)
    arrived(qr, pair_recv.at[1])
    got = (got + qr[...].astype(f32)) * inverse
    cosine, sine = cos_ref[...], sin_ref[...]
    size = cosine.shape[1]
    heads = wq.shape[1] // size

    def rotated(v):
        return (v * cosine + pltpu.roll(v, size // 2, 1) * sine).astype(bf16).astype(f32)

    for h in range(heads):
        q = rotated(got[:, h * size:(h + 1) * size])
        for s in range(2):
            q3[:, s * heads + h, :] = q[s * rows:(s + 1) * rows]
    k_new = rotated(got[:, heads * size:(heads + 1) * size])
    v_new = got[:, (heads + 1) * size:(heads + 2) * size].astype(bf16).astype(f32)
    if last > 1:
        out_step(1)

    key_load.wait()
    value_load.wait()
    scale = size ** -0.5
    slots = kc.shape[1]
    lane = lax.broadcasted_iota(jnp.int32, (CHUNK, 2 * heads, slots), 2)
    step_of = lax.broadcasted_iota(jnp.int32, (CHUNK, 2 * heads, 1), 1)
    for r0 in range(0, rows, CHUNK):
        if r0 == rows // 2 and last > 2:
            out_step(2)
        part = slice(r0, r0 + CHUNK)
        q = q3[part]
        scores = lax.dot_general(
            q.astype(bf16), kc[part], (((2,), (2,)), ((0,), (0,))), preferred_element_type=f32
        ) * scale
        live = live_ref[part][:, None, :]
        scores = jnp.where(lane < live, scores, -jnp.inf)
        k0, k1 = k_new[r0:r0 + CHUNK][:, None, :], k_new[rows + r0:rows + r0 + CHUNK][:, None, :]
        v0, v1 = v_new[r0:r0 + CHUNK][:, None, :], v_new[rows + r0:rows + r0 + CHUNK][:, None, :]
        n0 = jnp.sum(q * k0, axis=2, keepdims=True) * scale
        n1 = jnp.sum(q * k1, axis=2, keepdims=True) * scale
        n1 = jnp.where(step_of >= heads, n1, -jnp.inf)
        top = jnp.maximum(jnp.max(scores, axis=2, keepdims=True), jnp.maximum(n0, n1))
        probs = jnp.exp(scores - top)
        e0, e1 = jnp.exp(n0 - top), jnp.exp(n1 - top)
        total = jnp.sum(probs, axis=2, keepdims=True) + e0 + e1
        mixed = lax.dot_general(
            probs.astype(bf16), vc[part], (((2,), (1,)), ((0,), (0,))), preferred_element_type=f32
        )
        mixed = mixed + e0.astype(bf16).astype(f32) * v0 + e1.astype(bf16).astype(f32) * v1
        att3[part] = mixed / total
    attended = jnp.concatenate(
        [
            jnp.concatenate([att3[:, s * heads + h, :] for h in range(heads)], axis=1)
            for s in range(2)
        ],
        axis=0,
    ).astype(bf16)
    order = one_hot_rows(
        (2, NZ, 2, NX), lambda r_, z_, s_, x_: s_ * rows + r_ * half + z_ * NX + x_
    )
    attb[yl] = pick(order, attended).astype(bf16)
    send(attb.at[yl], attb.at[yl], pair_send.at[2], pair_recv.at[2], partner)

    a_wait(oa, 1, last)
    wait_spread(ob, 1)
    arrived(attb.at[1 - yl], pair_recv.at[2])
    full = attb[...].reshape(2 * both, heads * size)
    tiles = NYH // 2
    slab = NZ // tile_blocks

    def project(j):
        left = oa[pl.ds(j * slab, slab)].reshape(width, ocut)
        right = ob[pl.ds(j * slab, slab)].reshape(width, ob.shape[2])
        dims = (((1,), (1,)), ((), ()))
        return lax.dot_general(
            full[:, :ocut], left, dims, preferred_element_type=f32
        ) + lax.dot_general(full[:, ocut:], right, dims, preferred_element_type=f32)

    for i in range(tiles):
        ps[i] = project(2 * i + 1 - c).astype(bf16)
        send(ps.at[i], pr.at[i], core_send.at[i], core_recv.at[i], sib)
    for i in range(tiles):
        pk[i] = project(2 * i + c)
    for i in range(tiles):
        arrived(pr.at[i], core_recv.at[i])
        summed = (pk[i] + pr[i].astype(f32)).astype(bf16)
        for r in range(2):
            for g in range(2):
                lo = g * both + r * rows
                sp[i, r, g * rows:(g + 1) * rows, :] = summed[lo:lo + rows]
            is_self = jnp.logical_and(tiles * yl + i == yh, yl == r)
            there = dev(x, z, r, tiles * yl + i, c)
            away = remote(sp.at[i, r], rb.at[yh], y_send.at[2 * i + r], y_recv.at[yh], there)
            here = pltpu.make_async_copy(sp.at[i, r], rb.at[yh], y_recv.at[yh])
            pl.when(jnp.logical_not(is_self))(away.start)
            pl.when(is_self)(here.start)
    result = rr[...].reshape(both, width).astype(f32)
    for k in range(NYH):
        arrived(rb.at[k], y_recv.at[k])
        result = result + rb[k].astype(f32)

    result = result.reshape(2, NZ, 2 * NX, width)
    for k in range(NZ):
        zs[k] = jnp.concatenate([result[0, k], result[1, k]], axis=0).astype(bf16)
    zr[z] = zs[z]
    for d in range(1, NZ):
        zz = lax.rem(z + d, NZ)
        send(zs.at[zz], zr.at[z], za_send.at[d - 1], za_recv.at[d - 1], dev(x, zz, yl, yh, c))
    for d in range(1, NZ):
        arrived(zr.at[lax.rem(z + NZ - d, NZ)], za_recv.at[d - 1])
    order = one_hot_rows(
        (NX, 2, NZ, 2), lambda x_, g_, z_, s_: ((z_ * 2 + g_) * 2 + s_) * NX + x_
    )
    moved = pick(order, zr[...].reshape(both, width)).astype(bf16)
    xo[...] = moved.reshape(NX, 4 * NZ, width)
    xr[x] = xo[x]
    for d in range(1, NX):
        xx = lax.rem(x + d, NX)
        send(xo.at[xx], xr.at[x], xa_send.at[d - 1], xa_recv.at[d - 1], dev(xx, z, yl, yh, c))
    for d in range(1, NX):
        arrived(xr.at[lax.rem(x + NX - d, NX)], xa_recv.at[d - 1])
    order = one_hot_rows(
        (2, NZ, NX, 2), lambda g_, z_, x_, s_: ((x_ * 2 + g_) * NZ + z_) * 2 + s_
    )
    out[...] = pick(order, xr[...].reshape(both, width)).astype(bf16)

    for copy in sent:
        copy.wait_send()
    for s, buf in ((0, wb), (1, ob)):
        for d in range(1, NX):
            view = buf.at[:, mine]
            remote(view, view, bx_send.at[s, d - 1], bx_recv.at[s, d - 1], sib).wait_send()
    for k in range(NYH):
        is_self = jnp.logical_and(yl_to == yl, yh == k)
        away = remote(xs, xg.at[yl, tile_me], xs_send.at[k], xs_recv.at[src_me], sib)
        pl.when(jnp.logical_not(is_self))(away.wait_send)
        i, r = k // 2, k % 2
        is_self = jnp.logical_and(tiles * yl + i == yh, yl == r)
        away = remote(sp.at[i, r], rb.at[yh], y_send.at[k], y_recv.at[yh], sib)
        pl.when(jnp.logical_not(is_self))(away.wait_send)


def on_device(
    hidden, next_hidden, gain, w_query, w_key, w_value, w_out,
    key_cache, value_cache, lengths, positions,
):
    rows, width = hidden.shape
    both = 2 * rows
    slots, size = key_cache.shape[2], key_cache.shape[3]
    block, qcols = w_query.shape
    heads = qcols // size
    columns = qcols + 2 * size
    cut, ocut = columns // 2, qcols // 2
    half_width = NYH * width

    lane = jnp.arange(size, dtype=jnp.int32)
    place = (lane % (size // 2)).astype(f32)
    freqs = ROPE_BASE ** (-(2.0 * place) / size)
    where_at = jnp.concatenate([positions, positions + 1]).astype(f32)
    angle = where_at[:, None] * freqs[None, :]
    cosine = jnp.cos(angle)
    sine = jnp.sin(angle) * jnp.where(lane < size // 2, -1.0, 1.0)
    live = jnp.broadcast_to(lengths[:, None], (rows, slots))
    wide_gain = gain.astype(f32).reshape(2 * NYH, 1, width)

    vmem = pl.BlockSpec(memory_space=pltpu.VMEM)
    hbm = pl.BlockSpec(memory_space=pl.ANY)
    dma = lambda *shape: pltpu.SemaphoreType.DMA(shape)
    steps = NZ // 2
    result = pl.pallas_call(
        layer_kernel,
        out_shape=jax.ShapeDtypeStruct((both, width), bf16),
        in_specs=[vmem] * 10 + [hbm] * 2,
        out_specs=vmem,
        scratch_shapes=[
            pltpu.VMEM((NZ, NX * block, cut), bf16),
            pltpu.VMEM((NZ, NX * block, columns - cut), bf16),
            pltpu.VMEM((NZ, NX * block, ocut), bf16),
            pltpu.VMEM((NZ, NX * block, qcols - ocut), bf16),
            pltpu.VMEM((both, width), bf16),
            pltpu.VMEM((2, NYH, both, width), bf16),
            pltpu.VMEM((2, both, half_width), bf16),
            pltpu.VMEM((2, both, 128), f32),
            pltpu.VMEM((both, 128), f32),
            pltpu.VMEM((both, columns), bf16),
            pltpu.VMEM((both, columns), bf16),
            pltpu.VMEM((rows, slots, size), bf16),
            pltpu.VMEM((rows, slots, size), bf16),
            pltpu.VMEM((rows, 2 * heads, size), f32),
            pltpu.VMEM((rows, 2 * heads, size), f32),
            pltpu.VMEM((2, both, qcols), bf16),
            pltpu.VMEM((NYH // 2, 2 * both, width), bf16),
            pltpu.VMEM((NYH // 2, 2 * both, width), bf16),
            pltpu.VMEM((NYH // 2, 2 * both, width), f32),
            pltpu.VMEM((NYH // 2, 2, both, width), bf16),
            pltpu.VMEM((NYH, both, width), bf16),
            pltpu.VMEM((2, rows, width), bf16),
            pltpu.VMEM((NZ, 4 * NX, width), bf16),
            pltpu.VMEM((NZ, 4 * NX, width), bf16),
            pltpu.VMEM((NX, 4 * NZ, width), bf16),
            pltpu.VMEM((NX, 4 * NZ, width), bf16),
            dma(2),
            dma(NYH), dma(NYH), dma(NYH), dma(NYH), dma(2), dma(2),
            dma(2, NX - 1), dma(2, NX - 1), dma(2, 2, steps), dma(2, 2, steps),
            dma(2, NX - 1), dma(2, NX - 1), dma(2, 2, steps), dma(2, 2, steps),
            dma(3), dma(3), dma(NYH // 2), dma(NYH // 2), dma(NYH), dma(NYH),
            dma(NZ - 1), dma(NZ - 1), dma(NX - 1), dma(NX - 1),
        ],
        compiler_params=pltpu.CompilerParams(
            collective_id=0, has_side_effects=True, vmem_limit_bytes=56 * 1024 * 1024
        ),
        name="gathered_layer",
    )(
        hidden, next_hidden, wide_gain, w_query, w_key, w_value, w_out.T,
        cosine, sine, live,
        key_cache.reshape(rows, slots, size), value_cache.reshape(rows, slots, size),
    )
    return result.reshape(rows, 2, 1, width)


def solution(mesh):
    placed = (
        P("fsdp", "tp"),
        P("fsdp", "tp"),
        P(),
        P("fsdp", "tp"),
        P("fsdp", "tp"),
        P("fsdp", "tp"),
        P("tp", "fsdp"),
        P("fsdp", "tp", None, None),
        P("fsdp", "tp", None, None),
        P("fsdp"),
        P("fsdp"),
    )
    return jax.shard_map(
        on_device,
        mesh=mesh,
        in_specs=placed,
        out_specs=P(None, None, "fsdp", "tp"),
        check_vma=False,
    )
```

time: 1360 us -> 114 us (0.08)
  the two profiles are of different devices: /device:TPU:1 before, /device:TPU:16 now
where the time goes in v1:
time: 114 us
  Pallas kernels  107 us (94%)
  other arithmetic  3.67 us (3%)
  local copies, waits for them, and re-layouts  2.97 us (3%)
    pallas_call x1, Pallas kernels, on_device(): pl.pallas_call(layer_kernel, out_shape=jax.ShapeDtypeStruct((both, width)...  107 us

profile of v1, /device:TPU:16, one launch (start us, length us, event | category | flops | bytes accessed | tf_op | source)
XLA Modules:
  0.0 113.9 jit_solution(10437592578575749781)
XLA Ops:
  0.0 0.7 broadcast_add_fusion
  0.7 0.7 add_convert_fusion
  1.4 1.3 %reshape.54 = f32[5120]{0:T(1024)} convert(bf16[5120]{0:T(1024)(128)(2,1)} %param.13) | non-fusion elementwise | flops 5120 | bytes 30720 | tf_op jit(solution)/shard_map/reshape | solution.py:419
  2.7 1.3 %broadcast_in_dim.19.live_ref = s32[64,128]{1,0:T(8,128)} broadcast(s32[64]{0:T(128)} %param.20), dimensions={0} | broadcast | bytes 33024 | tf_op jit(solution)/shard_map/broadcast_in_dim | solution.py:418
  4.0 1.0 fusion
  5.0 107.2 %gathered_layer.1 = bf16[128,640]{1,0:T(8,128)(2,1)} custom-call(bf16[64,640]{1,0:T(8,128)(2,1)} %hid.1, bf16[64,640]{1,0:T(8,128)(2,1)} %nxt.1, f32[8,1,640]{2,1,0:T(1,128)} %bitcast.8, bf16[80,512]{1,0:T(8,128)(2,1)} %wq.1, bf16[80,128]{1,0:T(8,128)(2,1)} %wk.1, bf16[80,128]{1,0:T(8,128)(2,1)} %wv.1, bf16[80,512]{1,0:T(8,128)(2,1)} %bitcast.7, ...), custom_call_target="tpu_custom_call" | custom-call | tf_op jit(solution)/shard_map/gathered_layer/pallas_call | solution.py:425
  112.2 1.6 %reshape.53 = bf16[64,2,1,640]{3,1,0,2:T(2,128)(2,1)} reshape(bf16[128,640]{1,0:T(8,128)(2,1)} %gathered_layer.1) | data formatting | bytes 327680 | tf_op jit(solution)/shard_map/reshape | solution.py:473
  (1 shorter events, 0.0 us)

commit v2 on v1

--- a/solution.py
+++ b/solution.py
@@ -6,6 +6,7 @@
 from jax.experimental import pallas as pl
 from jax.experimental.pallas import tpu as pltpu
 from jax.sharding import PartitionSpec as P
+import numpy as np
 
 RMS_EPS = 1e-06
 ROPE_BASE = 1000000.0
@@ -36,13 +37,13 @@
 
 
 def layer_kernel(
-    hid, nxt, gain, wq, wk, wv, wot, cos_ref, sin_ref, live_ref, kc_hbm, vc_hbm,
+    hid, nxt, gain, wq, wk, wv, wot, freq_ref, len_ref, pos_ref, kc_hbm, vc_hbm,
     out,
     wa, wb, oa, ob, xs, xg, xn, ssb, ssr, qs, qr, kc, vc, q3, att3, attb,
-    ps, pr, pk, sp, rb, rr, zs, zr, xo, xr,
+    ps, pr, pk, sp, fb, rb, rr, zs, zr, xo, xr,
     cache_sem, xs_send, xs_recv, sib_send, sib_recv, res_send, res_recv,
-    ax_send, ax_recv, az_send, az_recv, bx_send, bx_recv, bz_send, bz_recv,
-    pair_send, pair_recv, core_send, core_recv, y_send, y_recv,
+    ax_send, ax_recv, az_send, az_recv, bx_send, bx_recv, bf_send, bf_recv, bz_send, bz_recv,
+    pair_send, pair_recv, core_send, core_recv, y_send, f_recv, y_recv,
     za_send, za_recv, xa_send, xa_recv,
 ):
     rows = hid.shape[0]
@@ -51,6 +52,7 @@
     width = hid.shape[1]
     block = wq.shape[0]
     tile_blocks = NYH
+    split = width // 256 * 128 + 128 if width >= 256 else width // 2
     f, t = lax.axis_index("fsdp"), lax.axis_index("tp")
     x, z, yl = lax.rem(f, NX), lax.rem(f // NX, NZ), f // (NX * NZ)
     yh, c = t // 2, lax.rem(t, 2)
@@ -160,21 +162,40 @@
         if k < last:
             arrived(buf.at[lax.rem(z + 1 + k, NZ), mine], bz_recv.at[s, 1, k])
 
+    x_up, x_down = lax.rem(x + 1, NX), lax.rem(x + NX - 1, NX)
+    beside = ((x_up, x_down), (x_down, x_up))[:min(2, NX - 1)]
+
+    def column(x_):
+        return pl.ds(pl.multiple_of(x_ * block, block), block)
+
+    def place(o):
+        return NZ // 2 * 2 - 1 if o == -NZ // 2 else (2 * o if o >= 0 else -2 * o - 1)
+
     def b_spread(buf, s, offsets):
         for o in offsets:
+            view = buf.at[lax.rem(z + NZ + o, NZ), mine]
+            for w, (to, _) in enumerate(beside):
+                send(view, view, bx_send.at[s, w, place(o)], bx_recv.at[s, w, place(o)],
+                     dev(to, z, yl, yh, c))
+
+    def b_relay(buf, s, offsets):
+        for o in offsets:
             zz = lax.rem(z + NZ + o, NZ)
-            for d in range(1, NX):
-                there = dev(lax.rem(x + d, NX), z, yl, yh, c)
-                remote(buf.at[zz, mine], buf.at[zz, mine],
-                       bx_send.at[s, d - 1], bx_recv.at[s, d - 1], there).start()
+            for w, (to, came) in enumerate(beside):
+                view = buf.at[zz, column(came)]
+                arrived(view, bx_recv.at[s, w, place(o)])
+                if NX == 4 and place(o) % 2 == w:
+                    send(view, view, bf_send.at[s, place(o)], bf_recv.at[s, place(o)],
+                         dev(to, z, yl, yh, c))
 
     def spread_after(k):
         return (-1 - k,) if k == last else (-1 - k, 1 + k)
 
-    def wait_spread(buf, s):
-        for d in range(1, NX):
-            xx = lax.rem(x + NX - d, NX)
-            arrived(buf.at[:, pl.ds(pl.multiple_of(xx * block, block), block)], bx_recv.at[s, d - 1])
+    def wait_relays(buf, s):
+        if NX == 4:
+            far = column(lax.rem(x + 2, NX))
+            for o in range(-NZ // 2, NZ // 2):
+                arrived(buf.at[lax.rem(z + NZ + o, NZ), far], bf_recv.at[s, place(o)])
 
     first_x(wa, 0)
     b_send(wb, 0, 0)
@@ -195,6 +216,7 @@
         b_wait(wb, 0, k)
         b_send(wb, 0, k + 1)
         b_spread(wb, 0, spread_after(k))
+        b_relay(wb, 0, spread_after(k - 1) if k else (0,))
         a_wait(wa, 0, k)
         a_send(wa, 0, k + 1)
 
@@ -204,17 +226,37 @@
         send(slot, slot, sib_send.at[k], sib_recv.at[k], sib)
     b_wait(wb, 0, last)
     b_spread(wb, 0, spread_after(last))
+    b_relay(wb, 0, spread_after(last - 1))
     for k in range(NYH):
         arrived(xg.at[k // (NYH // 2), (k % (NYH // 2)) * 2 + (1 - c)], sib_recv.at[k])
+
+    def scale_row(j):
+        start = pl.multiple_of((yl * tile_blocks + j) * width, width)
+        return gain[:, pl.ds(start, width)].astype(f32)
 
     for g in range(2):
         total = jnp.zeros((both, 1), f32)
         for j in range(tile_blocks):
             values = xg[g, j].astype(f32)
             total = total + jnp.sum(values * values, axis=1, keepdims=True)
-            xn[g, :, j * width:(j + 1) * width] = (values * gain[yl * tile_blocks + j]).astype(bf16)
+            xn[g, :, j * width:(j + 1) * width] = (values * scale_row(j)).astype(bf16)
         ssb[g] = jnp.broadcast_to(total, (both, 128))
     send(ssb.at[1 - yl], ssr, pair_send.at[0], pair_recv.at[0], partner)
+    b_relay(wb, 0, spread_after(last))
+
+    def as_column(row):
+        grid = (rows, rows)
+        diagonal = lax.broadcasted_iota(jnp.int32, grid, 0) == lax.broadcasted_iota(jnp.int32, grid, 1)
+        spread = jnp.broadcast_to(row[...].astype(f32), grid)
+        return jnp.sum(jnp.where(diagonal, spread, 0.0), axis=1, keepdims=True)
+
+    size = kc.shape[2]
+    first_at = as_column(pos_ref)
+    angle = jnp.concatenate([first_at, first_at + 1.0], axis=0) * freq_ref[...]
+    lane = lax.broadcasted_iota(jnp.int32, (both, size), 1)
+    cosine = jnp.cos(angle)
+    sine = jnp.where(lane < size // 2, -1.0, 1.0) * jnp.sin(angle)
+    live_rows = jnp.broadcast_to(as_column(len_ref), (rows, kc.shape[1]))
 
     for s in range(2):
         arrived(rr.at[1 - yl, pl.ds(s * half, half)], res_recv.at[s])
@@ -223,7 +265,7 @@
         rr[g] = pick(order, rr[g]).astype(bf16)
 
     a_wait(wa, 0, last)
-    wait_spread(wb, 0)
+    wait_relays(wb, 0)
     wait_first_x(oa, 1)
     a_send(oa, 1, 0)
     b_spread(ob, 1, (0,))
@@ -237,6 +279,7 @@
     qs[:, :cut] = jnp.dot(theirs, weight_a, preferred_element_type=f32).astype(bf16)
     qs[:, cut:] = jnp.dot(theirs, weight_b, preferred_element_type=f32).astype(bf16)
     send(qs, qr, pair_send.at[1], pair_recv.at[1], partner)
+    b_relay(ob, 1, (0,))
     ours = xn[yl]
     got_a = jnp.dot(ours, weight_a, preferred_element_type=f32)
     got_b = jnp.dot(ours, weight_b, preferred_element_type=f32)
@@ -249,6 +292,7 @@
         if k + 1 < last:
             b_send(ob, 1, k + 2)
         b_spread(ob, 1, spread_after(k + 1))
+        b_relay(ob, 1, spread_after(k))
 
     if last > 0:
         out_step(0)
@@ -257,8 +301,6 @@
     inverse = lax.rsqrt(square[:, :1] + RMS_EPS)
     arrived(qr, pair_recv.at[1])
     got = (got + qr[...].astype(f32)) * inverse
-    cosine, sine = cos_ref[...], sin_ref[...]
-    size = cosine.shape[1]
     heads = wq.shape[1] // size
 
     def rotated(v):
@@ -277,7 +319,7 @@
     value_load.wait()
     scale = size ** -0.5
     slots = kc.shape[1]
-    lane = lax.broadcasted_iota(jnp.int32, (CHUNK, 2 * heads, slots), 2)
+    lane = lax.broadcasted_iota(jnp.int32, (CHUNK, 2 * heads, slots), 2).astype(f32)
     step_of = lax.broadcasted_iota(jnp.int32, (CHUNK, 2 * heads, 1), 1)
     for r0 in range(0, rows, CHUNK):
         if r0 == rows // 2 and last > 2:
@@ -287,7 +329,7 @@
         scores = lax.dot_general(
             q.astype(bf16), kc[part], (((2,), (2,)), ((0,), (0,))), preferred_element_type=f32
         ) * scale
-        live = live_ref[part][:, None, :]
+        live = live_rows[part][:, None, :]
         scores = jnp.where(lane < live, scores, -jnp.inf)
         k0, k1 = k_new[r0:r0 + CHUNK][:, None, :], k_new[rows + r0:rows + r0 + CHUNK][:, None, :]
         v0, v1 = v_new[r0:r0 + CHUNK][:, None, :], v_new[rows + r0:rows + r0 + CHUNK][:, None, :]
@@ -316,8 +358,9 @@
     attb[yl] = pick(order, attended).astype(bf16)
     send(attb.at[yl], attb.at[yl], pair_send.at[2], pair_recv.at[2], partner)
 
+    b_relay(ob, 1, spread_after(last))
     a_wait(oa, 1, last)
-    wait_spread(ob, 1)
+    wait_relays(ob, 1)
     arrived(attb.at[1 - yl], pair_recv.at[2])
     full = attb[...].reshape(2 * both, heads * size)
     tiles = NYH // 2
@@ -342,57 +385,94 @@
         for r in range(2):
             for g in range(2):
                 lo = g * both + r * rows
-                sp[i, r, g * rows:(g + 1) * rows, :] = summed[lo:lo + rows]
-            is_self = jnp.logical_and(tiles * yl + i == yh, yl == r)
-            there = dev(x, z, r, tiles * yl + i, c)
-            away = remote(sp.at[i, r], rb.at[yh], y_send.at[2 * i + r], y_recv.at[yh], there)
-            here = pltpu.make_async_copy(sp.at[i, r], rb.at[yh], y_recv.at[yh])
-            pl.when(jnp.logical_not(is_self))(away.start)
-            pl.when(is_self)(here.start)
-    result = rr[...].reshape(both, width).astype(f32)
-    for k in range(NYH):
-        arrived(rb.at[k], y_recv.at[k])
-        result = result + rb[k].astype(f32)
-
-    result = result.reshape(2, NZ, 2 * NX, width)
-    for k in range(NZ):
-        zs[k] = jnp.concatenate([result[0, k], result[1, k]], axis=0).astype(bf16)
-    zr[z] = zs[z]
-    for d in range(1, NZ):
-        zz = lax.rem(z + d, NZ)
-        send(zs.at[zz], zr.at[z], za_send.at[d - 1], za_recv.at[d - 1], dev(x, zz, yl, yh, c))
-    for d in range(1, NZ):
-        arrived(zr.at[lax.rem(z + NZ - d, NZ)], za_recv.at[d - 1])
+                sp[2 * i + r, g * rows:(g + 1) * rows, :] = summed[lo:lo + rows]
+
+    def at(yy):
+        yy = lax.rem(yy + ny, ny)
+        return dev(x, z, lax.rem(yy, 2), yy // 2, c)
+
+    def ahead(m):
+        return lax.rem(NYH * yl + m - y + 2 * ny, ny)
+
+    cuts = [pl.ds(0, split), pl.ds(split, width - split)]
+
+    def either(delta, *values):
+        hit = delta == values[0]
+        for value in values[1:]:
+            hit = jnp.logical_or(hit, delta == value)
+        return hit
+
+    def far_copy(m, h, to):
+        return remote(sp.at[m, :, cuts[h]], fb.at[m, :, cuts[h]], y_send.at[m, h], f_recv.at[m, h], to)
+
+    def near_copy(m, h, side, to):
+        return remote(sp.at[m, :, cuts[h]], rb.at[side, :, cuts[h]], y_send.at[m, h], y_recv.at[side, h], to)
+
+    for h in range(2):
+        for m in range(NYH):
+            delta = ahead(m)
+            pl.when(either(delta, 3, 4) if h == 0 else delta == 3)(far_copy(m, h, at(y + 2)).start)
+            pl.when(delta == 5 if h == 0 else either(delta, 4, 5))(far_copy(m, h, at(y - 2)).start)
+    for h in range(2):
+        for m in range(NYH):
+            delta = ahead(m)
+
+            @pl.when(either(delta, 1, 7, 2 if h == 0 else 6))
+            def _():
+                arrived(fb.at[m, :, cuts[h]], f_recv.at[m, h])
+                lanes = slice(0, split) if h == 0 else slice(split, width)
+                sp[m, :, lanes] = (sp[m, :, lanes].astype(f32) + fb[m, :, lanes].astype(f32)).astype(bf16)
+
+            pl.when(either(delta, 1, 2))(near_copy(m, h, 0, at(NYH * yl + m)).start)
+            pl.when(either(delta, 6, 7))(near_copy(m, h, 1, at(NYH * yl + m)).start)
+
+    holds = jnp.where(y // NYH == yl, 1.0, 0.0)
+    for h in range(2):
+        lanes = slice(0, split) if h == 0 else slice(split, width)
+        result = rr[:, :, lanes].reshape(both, -1).astype(f32)
+        result = result + sp[lax.rem(y, NYH), :, lanes].astype(f32) * holds
+        for side in range(2):
+            arrived(rb.at[side, :, cuts[h]], y_recv.at[side, h])
+            result = result + rb[side, :, lanes].astype(f32)
+        result = result.reshape(2, NZ, 2 * NX, result.shape[1])
+        for k in range(NZ):
+            zs[k, :, lanes] = jnp.concatenate([result[0, k], result[1, k]], axis=0).astype(bf16)
+        zr[z, :, lanes] = zs[z, :, lanes]
+        for d in range(1, NZ):
+            zz = lax.rem(z + d, NZ)
+            send(zs.at[zz, :, cuts[h]], zr.at[z, :, cuts[h]], za_send.at[h, d - 1], za_recv.at[h, d - 1],
+                 dev(x, zz, yl, yh, c))
     order = one_hot_rows(
         (NX, 2, NZ, 2), lambda x_, g_, z_, s_: ((z_ * 2 + g_) * 2 + s_) * NX + x_
     )
-    moved = pick(order, zr[...].reshape(both, width)).astype(bf16)
-    xo[...] = moved.reshape(NX, 4 * NZ, width)
-    xr[x] = xo[x]
-    for d in range(1, NX):
-        xx = lax.rem(x + d, NX)
-        send(xo.at[xx], xr.at[x], xa_send.at[d - 1], xa_recv.at[d - 1], dev(xx, z, yl, yh, c))
-    for d in range(1, NX):
-        arrived(xr.at[lax.rem(x + NX - d, NX)], xa_recv.at[d - 1])
+    for h in range(2):
+        lanes = slice(0, split) if h == 0 else slice(split, width)
+        for d in range(1, NZ):
+            arrived(zr.at[lax.rem(z + NZ - d, NZ), :, cuts[h]], za_recv.at[h, d - 1])
+        moved = pick(order, zr[:, :, lanes].reshape(both, -1)).astype(bf16)
+        xo[:, :, lanes] = moved.reshape(NX, 4 * NZ, moved.shape[1])
+        xr[x, :, lanes] = xo[x, :, lanes]
+        for d in range(1, NX):
+            xx = lax.rem(x + d, NX)
+            send(xo.at[xx, :, cuts[h]], xr.at[x, :, cuts[h]], xa_send.at[h, d - 1], xa_recv.at[h, d - 1],
+                 dev(xx, z, yl, yh, c))
     order = one_hot_rows(
         (2, NZ, NX, 2), lambda g_, z_, x_, s_: ((x_ * 2 + g_) * NZ + z_) * 2 + s_
     )
-    out[...] = pick(order, xr[...].reshape(both, width)).astype(bf16)
+    for h in range(2):
+        lanes = slice(0, split) if h == 0 else slice(split, width)
+        for d in range(1, NX):
+            arrived(xr.at[lax.rem(x + NX - d, NX), :, cuts[h]], xa_recv.at[h, d - 1])
+        out[:, lanes] = pick(order, xr[:, :, lanes].reshape(both, -1)).astype(bf16)
 
     for copy in sent:
         copy.wait_send()
-    for s, buf in ((0, wb), (1, ob)):
-        for d in range(1, NX):
-            view = buf.at[:, mine]
-            remote(view, view, bx_send.at[s, d - 1], bx_recv.at[s, d - 1], sib).wait_send()
     for k in range(NYH):
         is_self = jnp.logical_and(yl_to == yl, yh == k)
         away = remote(xs, xg.at[yl, tile_me], xs_send.at[k], xs_recv.at[src_me], sib)
         pl.when(jnp.logical_not(is_self))(away.wait_send)
-        i, r = k // 2, k % 2
-        is_self = jnp.logical_and(tiles * yl + i == yh, yl == r)
-        away = remote(sp.at[i, r], rb.at[yh], y_send.at[k], y_recv.at[yh], sib)
-        pl.when(jnp.logical_not(is_self))(away.wait_send)
+        for h in range(2):
+            pl.when(ahead(k) != 0)(far_copy(k, h, sib).wait_send)
 
 
 def on_device(
@@ -408,15 +488,8 @@
     cut, ocut = columns // 2, qcols // 2
     half_width = NYH * width
 
-    lane = jnp.arange(size, dtype=jnp.int32)
-    place = (lane % (size // 2)).astype(f32)
-    freqs = ROPE_BASE ** (-(2.0 * place) / size)
-    where_at = jnp.concatenate([positions, positions + 1]).astype(f32)
-    angle = where_at[:, None] * freqs[None, :]
-    cosine = jnp.cos(angle)
-    sine = jnp.sin(angle) * jnp.where(lane < size // 2, -1.0, 1.0)
-    live = jnp.broadcast_to(lengths[:, None], (rows, slots))
-    wide_gain = gain.astype(f32).reshape(2 * NYH, 1, width)
+    place = np.arange(size) % (size // 2)
+    freqs = (ROPE_BASE ** (-(2.0 * place) / size)).astype(np.float32)[None, :]
 
     vmem = pl.BlockSpec(memory_space=pltpu.VMEM)
     hbm = pl.BlockSpec(memory_space=pl.ANY)
@@ -447,8 +520,9 @@
             pltpu.VMEM((NYH // 2, 2 * both, width), bf16),
             pltpu.VMEM((NYH // 2, 2 * both, width), bf16),
             pltpu.VMEM((NYH // 2, 2 * both, width), f32),
-            pltpu.VMEM((NYH // 2, 2, both, width), bf16),
             pltpu.VMEM((NYH, both, width), bf16),
+            pltpu.VMEM((NYH, both, width), bf16),
+            pltpu.VMEM((2, both, width), bf16),
             pltpu.VMEM((2, rows, width), bf16),
             pltpu.VMEM((NZ, 4 * NX, width), bf16),
             pltpu.VMEM((NZ, 4 * NX, width), bf16),
@@ -457,17 +531,17 @@
             dma(2),
             dma(NYH), dma(NYH), dma(NYH), dma(NYH), dma(2), dma(2),
             dma(2, NX - 1), dma(2, NX - 1), dma(2, 2, steps), dma(2, 2, steps),
-            dma(2, NX - 1), dma(2, NX - 1), dma(2, 2, steps), dma(2, 2, steps),
-            dma(3), dma(3), dma(NYH // 2), dma(NYH // 2), dma(NYH), dma(NYH),
-            dma(NZ - 1), dma(NZ - 1), dma(NX - 1), dma(NX - 1),
+            dma(2, 2, NZ), dma(2, 2, NZ), dma(2, NZ), dma(2, NZ), dma(2, 2, steps), dma(2, 2, steps),
+            dma(3), dma(3), dma(NYH // 2), dma(NYH // 2), dma(NYH, 2), dma(NYH, 2), dma(2, 2),
+            dma(2, NZ - 1), dma(2, NZ - 1), dma(2, NX - 1), dma(2, NX - 1),
         ],
         compiler_params=pltpu.CompilerParams(
             collective_id=0, has_side_effects=True, vmem_limit_bytes=56 * 1024 * 1024
         ),
         name="gathered_layer",
     )(
-        hidden, next_hidden, wide_gain, w_query, w_key, w_value, w_out.T,
-        cosine, sine, live,
+        hidden, next_hidden, gain[None, :], w_query, w_key, w_value, w_out.T,
+        jnp.asarray(freqs), lengths[None, :], positions[None, :],
         key_cache.reshape(rows, slots, size), value_cache.reshape(rows, slots, size),
     )
     return result.reshape(rows, 2, 1, width)

time: 114 us -> 114 us (level)
  the two profiles are of different devices: /device:TPU:16 before, /device:TPU:1 now
where the time goes in v2:
time: 114 us; the launch traced here: 113 us
  Pallas kernels  110 us (96%)
  local copies, waits for them, and re-layouts  2.96 us (3%)
    pallas_call x1, Pallas kernels, on_device(): pl.pallas_call(layer_kernel, out_shape=jax.ShapeDtypeStruct((both, width)...  110 us

profile of v2, /device:TPU:1, one launch (start us, length us, event | category | flops | bytes accessed | tf_op | source)
XLA Modules:
  0.0 113.3 jit_solution(11606900420046399176)
XLA Ops:
  0.0 1.3 %broadcast_in_dim.9.gain = bf16[1,5120]{1,0:T(2,128)(2,1)} reshape(bf16[5120]{0:T(1024)(128)(2,1)} %param.14) | data formatting | bytes 20480 | tf_op jit(solution)/shard_map/broadcast_in_dim | solution.py:543
  1.3 110.4 %gathered_layer.1 = bf16[128,640]{1,0:T(8,128)(2,1)} custom-call(bf16[64,640]{1,0:T(8,128)(2,1)} %hid.1, bf16[64,640]{1,0:T(8,128)(2,1)} %nxt.1, bf16[1,5120]{1,0:T(2,128)(2,1)} %broadcast_in_dim.9.gain, bf16[80,512]{1,0:T(8,128)(2,1)} %wq.1, bf16[80,128]{1,0:T(8,128)(2,1)} %wk.1, bf16[80,128]{1,0:T(8,128)(2,1)} %wv.1, bf16[80,512]{1,0:T(8,128)(2,1)} %bitcast.8, ...), custom_call_target="tpu_custom_call" | custom-call | tf_op jit(solution)/shard_map/gathered_layer/pallas_call | solution.py:498
  111.7 1.6 %reshape.11 = bf16[64,2,1,640]{3,1,0,2:T(2,128)(2,1)} reshape(bf16[128,640]{1,0:T(8,128)(2,1)} %gathered_layer.1) | data formatting | bytes 327680 | tf_op jit(solution)/shard_map/reshape | solution.py:547

commit v3 on v2

--- a/solution.py
+++ b/solution.py
@@ -39,10 +39,10 @@
 def layer_kernel(
     hid, nxt, gain, wq, wk, wv, wot, freq_ref, len_ref, pos_ref, kc_hbm, vc_hbm,
     out,
-    wa, wb, oa, ob, xs, xg, xn, ssb, ssr, qs, qr, kc, vc, q3, att3, attb,
-    ps, pr, pk, sp, fb, rb, rr, zs, zr, xo, xr,
+    wa, wb, oa, ob, xs, xg, xn, wide, ssb, ssr, qs, qr, kc, vc, q3, att3, attb,
+    ps, pr, sp, fb, rb, rr, zs, zr, xo, xr,
     cache_sem, xs_send, xs_recv, sib_send, sib_recv, res_send, res_recv,
-    ax_send, ax_recv, az_send, az_recv, bx_send, bx_recv, bf_send, bf_recv, bz_send, bz_recv,
+    ax_send, ax_recv, az_send, az_recv, bx_send, bx_recv, bz_send, bz_recv,
     pair_send, pair_recv, core_send, core_recv, y_send, f_recv, y_recv,
     za_send, za_recv, xa_send, xa_recv,
 ):
@@ -122,84 +122,96 @@
     down = dev(x, lax.rem(z + NZ - 1, NZ), yl, yh, c)
     last = NZ // 2 - 1
 
+    turns = tuple(range(NX)) if NX < 4 else (0, 1, 3, 2)
+
+    def column(e):
+        return pl.ds(pl.multiple_of(lax.rem(x + e, NX) * block, block), block)
+
+    def plane(o):
+        return lax.rem(z + NZ + o, NZ)
+
     def first_x(buf, s):
         for d in range(1, NX):
             there = dev(lax.rem(x + d, NX), z, yl, yh, c)
             send(buf.at[z, mine], buf.at[z, mine], ax_send.at[s, d - 1], ax_recv.at[s, d - 1], there)
 
-    def wait_first_x(buf, s):
-        for d in range(1, NX):
-            xx = lax.rem(x + NX - d, NX)
-            arrived(buf.at[z, pl.ds(pl.multiple_of(xx * block, block), block)], ax_recv.at[s, d - 1])
-
-    def slab_parts(k):
-        if k == last:
-            h = NX * block // 2
-            return pl.ds(0, h), pl.ds(h, h)
-        return pl.ds(0, NX * block), pl.ds(0, NX * block)
-
-    def a_send(buf, s, k):
-        p_up, p_down = slab_parts(k)
-        zz = lax.rem(z + NZ - k, NZ)
-        send(buf.at[zz, p_up], buf.at[zz, p_up], az_send.at[s, 0, k], az_recv.at[s, 0, k], up)
-        zz = lax.rem(z + k, NZ)
-        send(buf.at[zz, p_down], buf.at[zz, p_down], az_send.at[s, 1, k], az_recv.at[s, 1, k], down)
-
-    def a_wait(buf, s, k):
-        p_up, p_down = slab_parts(k)
-        arrived(buf.at[lax.rem(z + NZ - 1 - k, NZ), p_up], az_recv.at[s, 0, k])
-        arrived(buf.at[lax.rem(z + 1 + k, NZ), p_down], az_recv.at[s, 1, k])
+    def carried(k, w, i):
+        return k < last or (i < NX // 2) == (w == 0)
+
+    def a_send(buf, s, k, i):
+        for w, (to, zz) in enumerate(((up, plane(-k)), (down, plane(k)))):
+            if carried(k, w, i):
+                view = buf.at[zz, column(turns[i])]
+                send(view, view, az_send.at[s, w, k, i], az_recv.at[s, w, k, i], to)
+
+    def a_wait(buf, s, k, i):
+        for w, zz in enumerate((plane(-1 - k), plane(1 + k))):
+            if carried(k, w, i):
+                arrived(buf.at[zz, column(turns[i])], az_recv.at[s, w, k, i])
 
     def b_send(buf, s, k):
-        zz = lax.rem(z + NZ - k, NZ)
-        send(buf.at[zz, mine], buf.at[zz, mine], bz_send.at[s, 0, k], bz_recv.at[s, 0, k], up)
-        if k < last:
-            zz = lax.rem(z + k, NZ)
-            send(buf.at[zz, mine], buf.at[zz, mine], bz_send.at[s, 1, k], bz_recv.at[s, 1, k], down)
+        for w, (to, zz) in enumerate(((up, plane(-k)), (down, plane(k)))):
+            if k < last or w == 0:
+                send(buf.at[zz, mine], buf.at[zz, mine], bz_send.at[s, w, k], bz_recv.at[s, w, k], to)
 
     def b_wait(buf, s, k):
-        arrived(buf.at[lax.rem(z + NZ - 1 - k, NZ), mine], bz_recv.at[s, 0, k])
-        if k < last:
-            arrived(buf.at[lax.rem(z + 1 + k, NZ), mine], bz_recv.at[s, 1, k])
-
-    x_up, x_down = lax.rem(x + 1, NX), lax.rem(x + NX - 1, NX)
-    beside = ((x_up, x_down), (x_down, x_up))[:min(2, NX - 1)]
-
-    def column(x_):
-        return pl.ds(pl.multiple_of(x_ * block, block), block)
-
-    def place(o):
-        return NZ // 2 * 2 - 1 if o == -NZ // 2 else (2 * o if o >= 0 else -2 * o - 1)
+        for w, zz in enumerate((plane(-1 - k), plane(1 + k))):
+            if k < last or w == 0:
+                arrived(buf.at[zz, mine], bz_recv.at[s, w, k])
 
     def b_spread(buf, s, offsets):
         for o in offsets:
-            view = buf.at[lax.rem(z + NZ + o, NZ), mine]
-            for w, (to, _) in enumerate(beside):
-                send(view, view, bx_send.at[s, w, place(o)], bx_recv.at[s, w, place(o)],
-                     dev(to, z, yl, yh, c))
-
-    def b_relay(buf, s, offsets):
-        for o in offsets:
-            zz = lax.rem(z + NZ + o, NZ)
-            for w, (to, came) in enumerate(beside):
-                view = buf.at[zz, column(came)]
-                arrived(view, bx_recv.at[s, w, place(o)])
-                if NX == 4 and place(o) % 2 == w:
-                    send(view, view, bf_send.at[s, place(o)], bf_recv.at[s, place(o)],
-                         dev(to, z, yl, yh, c))
-
-    def spread_after(k):
-        return (-1 - k,) if k == last else (-1 - k, 1 + k)
-
-    def wait_relays(buf, s):
-        if NX == 4:
-            far = column(lax.rem(x + 2, NX))
-            for o in range(-NZ // 2, NZ // 2):
-                arrived(buf.at[lax.rem(z + NZ + o, NZ), far], bf_recv.at[s, place(o)])
-
-    first_x(wa, 0)
-    b_send(wb, 0, 0)
-    b_spread(wb, 0, (0,))
+            for d in range(1, NX):
+                there = dev(lax.rem(x + d, NX), z, yl, yh, c)
+                view = buf.at[plane(o), mine]
+                remote(view, view, bx_send.at[s, d - 1], bx_recv.at[s, d - 1], there).start()
+
+    def wait_spread(buf, s):
+        for d in range(1, NX):
+            arrived(buf.at[:, column(NX - d)], bx_recv.at[s, d - 1])
+
+    def stream(a_buf, b_buf, s):
+        def start():
+            a_send(a_buf, s, 0, 0)
+            b_send(b_buf, s, 0)
+            first_x(a_buf, s)
+            b_spread(b_buf, s, (0,))
+
+        def from_x(i):
+            arrived(a_buf.at[z, column(turns[i])], ax_recv.at[s, NX - turns[i] - 1])
+            a_send(a_buf, s, 0, i)
+
+        def b_step(k):
+            b_wait(b_buf, s, k)
+            if k < last:
+                b_send(b_buf, s, k + 1)
+            b_spread(b_buf, s, (-1 - k,) if k == last else (-1 - k, 1 + k))
+
+        def a_step(k, i):
+            a_wait(a_buf, s, k, i)
+            a_send(a_buf, s, k + 1, i)
+
+        steps = [start]
+        steps += [functools.partial(from_x, i) for i in range(1, NX)]
+        for k in range(last + 1):
+            steps.append(functools.partial(b_step, k))
+            if k < last:
+                steps += [functools.partial(a_step, k, i) for i in range(NX)]
+        return steps
+
+    def stream_end(a_buf, b_buf, s):
+        for i in range(NX):
+            a_wait(a_buf, s, last, i)
+        wait_spread(b_buf, s)
+
+    out_steps = stream(oa, ob, 1)
+
+    def pump(count):
+        for _ in range(min(count, len(out_steps))):
+            out_steps.pop(0)()
+
+    in_steps = stream(wa, wb, 0)
+    in_steps.pop(0)()
 
     away_rows = half * (1 - yl)
     own_rows = half * yl
@@ -208,49 +220,40 @@
         send(src, rr.at[yl, pl.ds(s * half, half)], res_send.at[s], res_recv.at[s], partner)
         rr[yl, s * half:(s + 1) * half, :] = xs[pl.ds(pl.multiple_of(s * rows + own_rows, half), half), :]
 
-    wait_first_x(wa, 0)
-    a_send(wa, 0, 0)
-    first_x(oa, 1)
-    b_send(ob, 1, 0)
-    for k in range(last):
-        b_wait(wb, 0, k)
-        b_send(wb, 0, k + 1)
-        b_spread(wb, 0, spread_after(k))
-        b_relay(wb, 0, spread_after(k - 1) if k else (0,))
-        a_wait(wa, 0, k)
-        a_send(wa, 0, k + 1)
+    def as_column(row):
+        grid = (rows, rows)
+        diagonal = lax.broadcasted_iota(jnp.int32, grid, 0) == lax.broadcasted_iota(jnp.int32, grid, 1)
+        spread = jnp.broadcast_to(row[...].astype(f32), grid)
+        return jnp.sum(jnp.where(diagonal, spread, 0.0), axis=1, keepdims=True)
+
+    size = kc.shape[2]
+    for step in in_steps:
+        step()
 
     for k in range(NYH):
         slot = xg.at[k // (NYH // 2), (k % (NYH // 2)) * 2 + c]
         arrived(slot, xs_recv.at[k])
         send(slot, slot, sib_send.at[k], sib_recv.at[k], sib)
-    b_wait(wb, 0, last)
-    b_spread(wb, 0, spread_after(last))
-    b_relay(wb, 0, spread_after(last - 1))
+    pump(1)
     for k in range(NYH):
         arrived(xg.at[k // (NYH // 2), (k % (NYH // 2)) * 2 + (1 - c)], sib_recv.at[k])
 
-    def scale_row(j):
-        start = pl.multiple_of((yl * tile_blocks + j) * width, width)
-        return gain[:, pl.ds(start, width)].astype(f32)
-
+    wide[...] = gain[...].astype(f32)
+    piece = min(128, width)
     for g in range(2):
         total = jnp.zeros((both, 1), f32)
         for j in range(tile_blocks):
             values = xg[g, j].astype(f32)
             total = total + jnp.sum(values * values, axis=1, keepdims=True)
-            xn[g, :, j * width:(j + 1) * width] = (values * scale_row(j)).astype(bf16)
+            for p in range(width // piece):
+                row = (yl * tile_blocks + j) * (width // piece) + p
+                xn[g, :, j * width + p * piece:j * width + (p + 1) * piece] = (
+                    values[:, p * piece:(p + 1) * piece] * wide[pl.ds(row, 1), :]
+                ).astype(bf16)
         ssb[g] = jnp.broadcast_to(total, (both, 128))
     send(ssb.at[1 - yl], ssr, pair_send.at[0], pair_recv.at[0], partner)
-    b_relay(wb, 0, spread_after(last))
-
-    def as_column(row):
-        grid = (rows, rows)
-        diagonal = lax.broadcasted_iota(jnp.int32, grid, 0) == lax.broadcasted_iota(jnp.int32, grid, 1)
-        spread = jnp.broadcast_to(row[...].astype(f32), grid)
-        return jnp.sum(jnp.where(diagonal, spread, 0.0), axis=1, keepdims=True)
-
-    size = kc.shape[2]
+    pump(2)
+
     first_at = as_column(pos_ref)
     angle = jnp.concatenate([first_at, first_at + 1.0], axis=0) * freq_ref[...]
     lane = lax.broadcasted_iota(jnp.int32, (both, size), 1)
@@ -264,42 +267,29 @@
     for g in range(2):
         rr[g] = pick(order, rr[g]).astype(bf16)
 
-    a_wait(wa, 0, last)
-    wait_relays(wb, 0)
-    wait_first_x(oa, 1)
-    a_send(oa, 1, 0)
-    b_spread(ob, 1, (0,))
-    b_wait(ob, 1, 0)
-    b_send(ob, 1, 1)
-    b_spread(ob, 1, spread_after(0))
+    pump(1)
+    stream_end(wa, wb, 0)
     depth = NZ * NX * block
     weight_a = wa[...].reshape(depth, cut)
     weight_b = wb[...].reshape(depth, wb.shape[2])
     theirs = xn[1 - yl]
     qs[:, :cut] = jnp.dot(theirs, weight_a, preferred_element_type=f32).astype(bf16)
+    send(qs.at[:, 0:cut], qr.at[:, 0:cut], pair_send.at[1], pair_recv.at[1], partner)
     qs[:, cut:] = jnp.dot(theirs, weight_b, preferred_element_type=f32).astype(bf16)
-    send(qs, qr, pair_send.at[1], pair_recv.at[1], partner)
-    b_relay(ob, 1, (0,))
+    rest = pl.ds(cut, qs.shape[1] - cut)
+    send(qs.at[:, rest], qr.at[:, rest], pair_send.at[3], pair_recv.at[3], partner)
+    pump(2)
     ours = xn[yl]
     got_a = jnp.dot(ours, weight_a, preferred_element_type=f32)
     got_b = jnp.dot(ours, weight_b, preferred_element_type=f32)
     got = jnp.concatenate([got_a, got_b], axis=1)
-
-    def out_step(k):
-        a_wait(oa, 1, k)
-        a_send(oa, 1, k + 1)
-        b_wait(ob, 1, k + 1)
-        if k + 1 < last:
-            b_send(ob, 1, k + 2)
-        b_spread(ob, 1, spread_after(k + 1))
-        b_relay(ob, 1, spread_after(k))
-
-    if last > 0:
-        out_step(0)
+    pump(2)
     arrived(ssr, pair_recv.at[0])
     square = (ssb[yl] + ssr[...]) * (1.0 / (2 * tile_blocks * width))
     inverse = lax.rsqrt(square[:, :1] + RMS_EPS)
-    arrived(qr, pair_recv.at[1])
+    arrived(qr.at[:, 0:cut], pair_recv.at[1])
+    arrived(qr.at[:, rest], pair_recv.at[3])
+    pump(1)
     got = (got + qr[...].astype(f32)) * inverse
     heads = wq.shape[1] // size
 
@@ -312,8 +302,7 @@
             q3[:, s * heads + h, :] = q[s * rows:(s + 1) * rows]
     k_new = rotated(got[:, heads * size:(heads + 1) * size])
     v_new = got[:, (heads + 1) * size:(heads + 2) * size].astype(bf16).astype(f32)
-    if last > 1:
-        out_step(1)
+    pump(2)
 
     key_load.wait()
     value_load.wait()
@@ -322,8 +311,7 @@
     lane = lax.broadcasted_iota(jnp.int32, (CHUNK, 2 * heads, slots), 2).astype(f32)
     step_of = lax.broadcasted_iota(jnp.int32, (CHUNK, 2 * heads, 1), 1)
     for r0 in range(0, rows, CHUNK):
-        if r0 == rows // 2 and last > 2:
-            out_step(2)
+        pump(2)
         part = slice(r0, r0 + CHUNK)
         q = q3[part]
         scores = lax.dot_general(
@@ -358,9 +346,8 @@
     attb[yl] = pick(order, attended).astype(bf16)
     send(attb.at[yl], attb.at[yl], pair_send.at[2], pair_recv.at[2], partner)
 
-    b_relay(ob, 1, spread_after(last))
-    a_wait(oa, 1, last)
-    wait_relays(ob, 1)
+    pump(len(out_steps))
+    stream_end(oa, ob, 1)
     arrived(attb.at[1 - yl], pair_recv.at[2])
     full = attb[...].reshape(2 * both, heads * size)
     tiles = NYH // 2
@@ -377,16 +364,6 @@
     for i in range(tiles):
         ps[i] = project(2 * i + 1 - c).astype(bf16)
         send(ps.at[i], pr.at[i], core_send.at[i], core_recv.at[i], sib)
-    for i in range(tiles):
-        pk[i] = project(2 * i + c)
-    for i in range(tiles):
-        arrived(pr.at[i], core_recv.at[i])
-        summed = (pk[i] + pr[i].astype(f32)).astype(bf16)
-        for r in range(2):
-            for g in range(2):
-                lo = g * both + r * rows
-                sp[2 * i + r, g * rows:(g + 1) * rows, :] = summed[lo:lo + rows]
-
     def at(yy):
         yy = lax.rem(yy + ny, ny)
         return dev(x, z, lax.rem(yy, 2), yy // 2, c)
@@ -408,23 +385,35 @@
     def near_copy(m, h, side, to):
         return remote(sp.at[m, :, cuts[h]], rb.at[side, :, cuts[h]], y_send.at[m, h], y_recv.at[side, h], to)
 
+    for i in range(tiles):
+        kept = project(2 * i + c)
+        arrived(pr.at[i], core_recv.at[i])
+        summed = (kept + pr[i].astype(f32)).astype(bf16)
+        for r in range(2):
+            for g in range(2):
+                lo = g * both + r * rows
+                sp[2 * i + r, g * rows:(g + 1) * rows, :] = summed[lo:lo + rows]
+        for h in range(2):
+            for m in (2 * i, 2 * i + 1):
+                delta = ahead(m)
+                pl.when(either(delta, 3, 4) if h == 0 else delta == 3)(far_copy(m, h, at(y + 2)).start)
+                pl.when(delta == 5 if h == 0 else either(delta, 4, 5))(far_copy(m, h, at(y - 2)).start)
+                if h == 0:
+                    pl.when(delta == 6)(near_copy(m, h, 1, at(NYH * yl + m)).start)
+                else:
+                    pl.when(delta == 2)(near_copy(m, h, 0, at(NYH * yl + m)).start)
     for h in range(2):
-        for m in range(NYH):
-            delta = ahead(m)
-            pl.when(either(delta, 3, 4) if h == 0 else delta == 3)(far_copy(m, h, at(y + 2)).start)
-            pl.when(delta == 5 if h == 0 else either(delta, 4, 5))(far_copy(m, h, at(y - 2)).start)
-    for h in range(2):
+        lanes = slice(0, split) if h == 0 else slice(split, width)
         for m in range(NYH):
             delta = ahead(m)
 
             @pl.when(either(delta, 1, 7, 2 if h == 0 else 6))
             def _():
                 arrived(fb.at[m, :, cuts[h]], f_recv.at[m, h])
-                lanes = slice(0, split) if h == 0 else slice(split, width)
                 sp[m, :, lanes] = (sp[m, :, lanes].astype(f32) + fb[m, :, lanes].astype(f32)).astype(bf16)
 
-            pl.when(either(delta, 1, 2))(near_copy(m, h, 0, at(NYH * yl + m)).start)
-            pl.when(either(delta, 6, 7))(near_copy(m, h, 1, at(NYH * yl + m)).start)
+            pl.when(either(delta, 1, 2) if h == 0 else delta == 1)(near_copy(m, h, 0, at(NYH * yl + m)).start)
+            pl.when(delta == 7 if h == 0 else either(delta, 6, 7))(near_copy(m, h, 1, at(NYH * yl + m)).start)
 
     holds = jnp.where(y // NYH == yl, 1.0, 0.0)
     for h in range(2):
@@ -467,6 +456,10 @@
 
     for copy in sent:
         copy.wait_send()
+    for s, buf in ((0, wb), (1, ob)):
+        for d in range(1, NX):
+            view = buf.at[:, mine]
+            remote(view, view, bx_send.at[s, d - 1], bx_recv.at[s, d - 1], sib).wait_send()
     for k in range(NYH):
         is_self = jnp.logical_and(yl_to == yl, yh == k)
         away = remote(xs, xg.at[yl, tile_me], xs_send.at[k], xs_recv.at[src_me], sib)
@@ -488,6 +481,7 @@
     cut, ocut = columns // 2, qcols // 2
     half_width = NYH * width
 
+    tall = gain.reshape(-1, min(128, width))
     place = np.arange(size) % (size // 2)
     freqs = (ROPE_BASE ** (-(2.0 * place) / size)).astype(np.float32)[None, :]
 
@@ -508,6 +502,7 @@
             pltpu.VMEM((both, width), bf16),
             pltpu.VMEM((2, NYH, both, width), bf16),
             pltpu.VMEM((2, both, half_width), bf16),
+            pltpu.VMEM(tall.shape, f32),
             pltpu.VMEM((2, both, 128), f32),
             pltpu.VMEM((both, 128), f32),
             pltpu.VMEM((both, columns), bf16),
@@ -519,7 +514,6 @@
             pltpu.VMEM((2, both, qcols), bf16),
             pltpu.VMEM((NYH // 2, 2 * both, width), bf16),
             pltpu.VMEM((NYH // 2, 2 * both, width), bf16),
-            pltpu.VMEM((NYH // 2, 2 * both, width), f32),
             pltpu.VMEM((NYH, both, width), bf16),
             pltpu.VMEM((NYH, both, width), bf16),
             pltpu.VMEM((2, both, width), bf16),
@@ -530,9 +524,9 @@
             pltpu.VMEM((NX, 4 * NZ, width), bf16),
             dma(2),
             dma(NYH), dma(NYH), dma(NYH), dma(NYH), dma(2), dma(2),
+            dma(2, NX - 1), dma(2, NX - 1), dma(2, 2, steps, NX), dma(2, 2, steps, NX),
             dma(2, NX - 1), dma(2, NX - 1), dma(2, 2, steps), dma(2, 2, steps),
-            dma(2, 2, NZ), dma(2, 2, NZ), dma(2, NZ), dma(2, NZ), dma(2, 2, steps), dma(2, 2, steps),
-            dma(3), dma(3), dma(NYH // 2), dma(NYH // 2), dma(NYH, 2), dma(NYH, 2), dma(2, 2),
+            dma(4), dma(4), dma(NYH // 2), dma(NYH // 2), dma(NYH, 2), dma(NYH, 2), dma(2, 2),
             dma(2, NZ - 1), dma(2, NZ - 1), dma(2, NX - 1), dma(2, NX - 1),
         ],
         compiler_params=pltpu.CompilerParams(
@@ -540,7 +534,7 @@
         ),
         name="gathered_layer",
     )(
-        hidden, next_hidden, gain[None, :], w_query, w_key, w_value, w_out.T,
+        hidden, next_hidden, tall, w_query, w_key, w_value, w_out.T,
         jnp.asarray(freqs), lengths[None, :], positions[None, :],
         key_cache.reshape(rows, slots, size), value_cache.reshape(rows, slots, size),
     )

time: 114 us -> 99.7 us (0.87)
  Pallas kernels: 110 us -> 97.9 us
  local copies, waits for them, and re-layouts: 2.96 us -> 1.65 us
    pallas_call x1, Pallas kernels: 110 us -> 97.9 us  [on_device(): pl.pallas_call(layer_kernel, out_shape=jax.ShapeDtypeStruct((both, width)...]
    broadcast_in_dim x1 -> x0, local copies, waits for them, and re-layouts: 1.32 us -> none  [on_device(): gain[None, :]]
where the time goes in v3:
time: 99.7 us; the launch traced here: 99.5 us
  Pallas kernels  97.9 us (98%)
  local copies, waits for them, and re-layouts  1.65 us (2%)
    pallas_call x1, Pallas kernels, on_device(): pl.pallas_call(layer_kernel, out_shape=jax.ShapeDtypeStruct((both, width)...  97.9 us

profile of v3, /device:TPU:1, one launch (start us, length us, event | category | flops | bytes accessed | tf_op | source)
XLA Modules:
  0.0 99.5 jit_solution(5495251016579777552)
XLA Ops:
  0.0 97.9 %gathered_layer.1 = bf16[128,640]{1,0:T(8,128)(2,1)} custom-call(bf16[64,640]{1,0:T(8,128)(2,1)} %hid.1, bf16[64,640]{1,0:T(8,128)(2,1)} %nxt.1, bf16[40,128]{1,0:T(8,128)(2,1)} %bitcast.10, bf16[80,512]{1,0:T(8,128)(2,1)} %wq.1, bf16[80,128]{1,0:T(8,128)(2,1)} %wk.1, bf16[80,128]{1,0:T(8,128)(2,1)} %wv.1, bf16[80,512]{1,0:T(8,128)(2,1)} %bitcast.9, ...), custom_call_target="tpu_custom_call" | custom-call | tf_op jit(solution)/shard_map/gathered_layer/pallas_call | solution.py:492
  97.9 1.6 %reshape.15 = bf16[64,2,1,640]{3,1,0,2:T(2,128)(2,1)} reshape(bf16[128,640]{1,0:T(8,128)(2,1)} %gathered_layer.1) | data formatting | bytes 327680 | tf_op jit(solution)/shard_map/reshape | solution.py:541

commit v4 on v3

--- a/solution.py
+++ b/solution.py
@@ -41,7 +41,7 @@
     out,
     wa, wb, oa, ob, xs, xg, xn, wide, ssb, ssr, qs, qr, kc, vc, q3, att3, attb,
     ps, pr, sp, fb, rb, rr, zs, zr, xo, xr,
-    cache_sem, xs_send, xs_recv, sib_send, sib_recv, res_send, res_recv,
+    cache_sem, xs_send, xr_send, xs_recv, sib_send, sib_recv, res_send, res_recv,
     ax_send, ax_recv, az_send, az_recv, bx_send, bx_recv, bz_send, bz_recv,
     pair_send, pair_recv, core_send, core_recv, y_send, f_recv, y_recv,
     za_send, za_recv, xa_send, xa_recv,
@@ -107,16 +107,74 @@
     xs[rows:both, :] = nxt[...]
     pl.semaphore_wait(barrier, len(places))
 
-    yl_to = yh // (NYH // 2)
+    def at(yy):
+        yy = lax.rem(yy + ny, ny)
+        return dev(x, z, lax.rem(yy, 2), yy // 2, c)
+
+    def either(delta, *values):
+        hit = delta == values[0]
+        for value in values[1:]:
+            hit = jnp.logical_or(hit, delta == value)
+        return hit
+
+    halves = (pl.ds(0, rows), pl.ds(rows, rows))
+    parity = y // NYH
     tile_me = lax.rem(yh, NYH // 2) * 2 + c
-    src_me = yl * (NYH // 2) + lax.rem(yh, NYH // 2)
+    src_me = lax.rem(y, NYH)
+
+    def input_slot(m, h):
+        return xg.at[m % 2, (m // 2) * 2 + c, halves[h]]
+
+    def input_away(k, h):
+        return remote(xs.at[halves[h]], xg.at[yl, tile_me, halves[h]],
+                      xs_send.at[k, h], xs_recv.at[src_me, h], at(2 * k + parity))
+
     for k in range(NYH):
-        is_self = jnp.logical_and(yl_to == yl, yh == k)
-        there = dev(x, z, yl_to, k, c)
-        away = remote(xs, xg.at[yl, tile_me], xs_send.at[k], xs_recv.at[src_me], there)
-        here = pltpu.make_async_copy(xs, xg.at[yl, tile_me], xs_recv.at[src_me])
-        pl.when(jnp.logical_not(is_self))(away.start)
-        pl.when(is_self)(here.start)
+        delta = lax.rem(2 * k + parity - y + ny, ny)
+        for h in range(2):
+            here = pltpu.make_async_copy(
+                xs.at[halves[h]], xg.at[yl, tile_me, halves[h]], xs_recv.at[src_me, h])
+            pl.when(either(delta, 1, 2, 6, 7))(input_away(k, h).start)
+            pl.when(delta == 0)(here.start)
+
+    def input_relay(m, h, to):
+        return remote(input_slot(m, h), input_slot(m, h), xr_send.at[m, h], xs_recv.at[m, h], to)
+
+    def relays(m, h):
+        delta = lax.rem(y - NYH * yl - m + 2 * ny, ny)
+        onward = either(delta, 1, 2) if h == 0 else delta == 1
+        back = delta == 7 if h == 0 else either(delta, 6, 7)
+        return onward, back
+
+    def to_sibling(m, h):
+        return remote(input_slot(m, h), input_slot(m, h), sib_send.at[m, h], sib_recv.at[m, h], sib)
+
+    def relay_inputs():
+        for m in range(NYH):
+            for h in range(2):
+                onward, back = relays(m, h)
+
+                @pl.when(jnp.logical_or(onward, back))
+                def _():
+                    arrived(input_slot(m, h), xs_recv.at[m, h])
+                    to_sibling(m, h).start()
+
+                pl.when(onward)(input_relay(m, h, at(y + 2)).start)
+                pl.when(back)(input_relay(m, h, at(y - 2)).start)
+
+    def end_inputs():
+        for m in range(NYH):
+            for h in range(2):
+                onward, back = relays(m, h)
+
+                @pl.when(jnp.logical_not(jnp.logical_or(onward, back)))
+                def _():
+                    arrived(input_slot(m, h), xs_recv.at[m, h])
+                    to_sibling(m, h).start()
+
+        for m in range(NYH):
+            for h in range(2):
+                arrived(xg.at[m % 2, (m // 2) * 2 + 1 - c, halves[h]], sib_recv.at[m, h])
 
     up = dev(x, lax.rem(z + 1, NZ), yl, yh, c)
     down = dev(x, lax.rem(z + NZ - 1, NZ), yl, yh, c)
@@ -191,12 +249,14 @@
             a_wait(a_buf, s, k, i)
             a_send(a_buf, s, k + 1, i)
 
-        steps = [start]
-        steps += [functools.partial(from_x, i) for i in range(1, NX)]
-        for k in range(last + 1):
-            steps.append(functools.partial(b_step, k))
-            if k < last:
-                steps += [functools.partial(a_step, k, i) for i in range(NX)]
+        firsts = [functools.partial(from_x, i) for i in range(1, NX)]
+        smalls = [functools.partial(b_step, k) for k in range(last + 1)]
+        larges = [functools.partial(a_step, k, i) for k in range(last) for i in range(NX)]
+        steps = [start] + firsts[:1] + smalls[:1] + firsts[1:]
+        for small in smalls[1:]:
+            steps += larges[:2] + [small]
+            larges = larges[2:]
+        steps += larges
         return steps
 
     def stream_end(a_buf, b_buf, s):
@@ -227,16 +287,13 @@
         return jnp.sum(jnp.where(diagonal, spread, 0.0), axis=1, keepdims=True)
 
     size = kc.shape[2]
-    for step in in_steps:
+    for number, step in enumerate(in_steps):
+        if number == 2 * NX:
+            relay_inputs()
         step()
 
-    for k in range(NYH):
-        slot = xg.at[k // (NYH // 2), (k % (NYH // 2)) * 2 + c]
-        arrived(slot, xs_recv.at[k])
-        send(slot, slot, sib_send.at[k], sib_recv.at[k], sib)
     pump(1)
-    for k in range(NYH):
-        arrived(xg.at[k // (NYH // 2), (k % (NYH // 2)) * 2 + (1 - c)], sib_recv.at[k])
+    end_inputs()
 
     wide[...] = gain[...].astype(f32)
     piece = min(128, width)
@@ -364,20 +421,10 @@
     for i in range(tiles):
         ps[i] = project(2 * i + 1 - c).astype(bf16)
         send(ps.at[i], pr.at[i], core_send.at[i], core_recv.at[i], sib)
-    def at(yy):
-        yy = lax.rem(yy + ny, ny)
-        return dev(x, z, lax.rem(yy, 2), yy // 2, c)
-
     def ahead(m):
         return lax.rem(NYH * yl + m - y + 2 * ny, ny)
 
     cuts = [pl.ds(0, split), pl.ds(split, width - split)]
-
-    def either(delta, *values):
-        hit = delta == values[0]
-        for value in values[1:]:
-            hit = jnp.logical_or(hit, delta == value)
-        return hit
 
     def far_copy(m, h, to):
         return remote(sp.at[m, :, cuts[h]], fb.at[m, :, cuts[h]], y_send.at[m, h], f_recv.at[m, h], to)
@@ -461,9 +508,11 @@
             view = buf.at[:, mine]
             remote(view, view, bx_send.at[s, d - 1], bx_recv.at[s, d - 1], sib).wait_send()
     for k in range(NYH):
-        is_self = jnp.logical_and(yl_to == yl, yh == k)
-        away = remote(xs, xg.at[yl, tile_me], xs_send.at[k], xs_recv.at[src_me], sib)
-        pl.when(jnp.logical_not(is_self))(away.wait_send)
+        for h in range(2):
+            delta = lax.rem(2 * k + parity - y + ny, ny)
+            pl.when(either(delta, 1, 2, 6, 7))(input_away(k, h).wait_send)
+            pl.when(jnp.logical_or(*relays(k, h)))(input_relay(k, h, sib).wait_send)
+            to_sibling(k, h).wait_send()
         for h in range(2):
             pl.when(ahead(k) != 0)(far_copy(k, h, sib).wait_send)
 
@@ -523,7 +572,7 @@
             pltpu.VMEM((NX, 4 * NZ, width), bf16),
             pltpu.VMEM((NX, 4 * NZ, width), bf16),
             dma(2),
-            dma(NYH), dma(NYH), dma(NYH), dma(NYH), dma(2), dma(2),
+            dma(NYH, 2), dma(NYH, 2), dma(NYH, 2), dma(NYH, 2), dma(NYH, 2), dma(2), dma(2),
             dma(2, NX - 1), dma(2, NX - 1), dma(2, 2, steps, NX), dma(2, 2, steps, NX),
             dma(2, NX - 1), dma(2, NX - 1), dma(2, 2, steps), dma(2, 2, steps),
             dma(4), dma(4), dma(NYH // 2), dma(NYH // 2), dma(NYH, 2), dma(NYH, 2), dma(2, 2),

time: 99.7 us -> 102 us (1.023)
  Pallas kernels: 97.9 us -> 100 us
    pallas_call x1, Pallas kernels: 97.9 us -> 100 us  [on_device(): pl.pallas_call(layer_kernel, out_shape=jax.ShapeDtypeStruct((both, width)...]
where the time goes in v4:
time: 102 us
  Pallas kernels  100 us (98%)
  local copies, waits for them, and re-layouts  1.65 us (2%)
    pallas_call x1, Pallas kernels, on_device(): pl.pallas_call(layer_kernel, out_shape=jax.ShapeDtypeStruct((both, width)...  100 us

profile of v4, /device:TPU:1, one launch (start us, length us, event | category | flops | bytes accessed | tf_op | source)
XLA Modules:
  0.0 101.9 jit_solution(17925830505945629419)
XLA Ops:
  0.0 100.2 %gathered_layer.1 = bf16[128,640]{1,0:T(8,128)(2,1)} custom-call(bf16[64,640]{1,0:T(8,128)(2,1)} %hid.1, bf16[64,640]{1,0:T(8,128)(2,1)} %nxt.1, bf16[40,128]{1,0:T(8,128)(2,1)} %bitcast.10, bf16[80,512]{1,0:T(8,128)(2,1)} %wq.1, bf16[80,128]{1,0:T(8,128)(2,1)} %wk.1, bf16[80,128]{1,0:T(8,128)(2,1)} %wv.1, bf16[80,512]{1,0:T(8,128)(2,1)} %bitcast.9, ...), custom_call_target="tpu_custom_call" | custom-call | tf_op jit(solution)/shard_map/gathered_layer/pallas_call | solution.py:541
  100.2 1.6 %reshape.15 = bf16[64,2,1,640]{3,1,0,2:T(2,128)(2,1)} reshape(bf16[128,640]{1,0:T(8,128)(2,1)} %gathered_layer.1) | data formatting | bytes 327680 | tf_op jit(solution)/shard_map/reshape | solution.py:590

commit v5 on v3

--- a/solution.py
+++ b/solution.py
@@ -164,11 +164,13 @@
             for d in range(1, NX):
                 there = dev(lax.rem(x + d, NX), z, yl, yh, c)
                 view = buf.at[plane(o), mine]
-                remote(view, view, bx_send.at[s, d - 1], bx_recv.at[s, d - 1], there).start()
-
-    def wait_spread(buf, s):
+                side = plane(o) // (NZ // 2)
+                remote(view, view, bx_send.at[s, d - 1], bx_recv.at[s, d - 1, side], there).start()
+
+    def wait_spread(buf, s, side):
         for d in range(1, NX):
-            arrived(buf.at[:, column(NX - d)], bx_recv.at[s, d - 1])
+            planes = pl.ds(pl.multiple_of(side * (NZ // 2), NZ // 2), NZ // 2)
+            arrived(buf.at[planes, column(NX - d)], bx_recv.at[s, d - 1, side])
 
     def stream(a_buf, b_buf, s):
         def start():
@@ -199,10 +201,9 @@
                 steps += [functools.partial(a_step, k, i) for i in range(NX)]
         return steps
 
-    def stream_end(a_buf, b_buf, s):
+    def last_blocks(a_buf, s):
         for i in range(NX):
             a_wait(a_buf, s, last, i)
-        wait_spread(b_buf, s)
 
     out_steps = stream(oa, ob, 1)
 
@@ -268,16 +269,18 @@
         rr[g] = pick(order, rr[g]).astype(bf16)
 
     pump(1)
-    stream_end(wa, wb, 0)
+    wait_spread(wb, 0, 0)
+    wait_spread(wb, 0, 1)
     depth = NZ * NX * block
-    weight_a = wa[...].reshape(depth, cut)
     weight_b = wb[...].reshape(depth, wb.shape[2])
     theirs = xn[1 - yl]
-    qs[:, :cut] = jnp.dot(theirs, weight_a, preferred_element_type=f32).astype(bf16)
-    send(qs.at[:, 0:cut], qr.at[:, 0:cut], pair_send.at[1], pair_recv.at[1], partner)
     qs[:, cut:] = jnp.dot(theirs, weight_b, preferred_element_type=f32).astype(bf16)
     rest = pl.ds(cut, qs.shape[1] - cut)
     send(qs.at[:, rest], qr.at[:, rest], pair_send.at[3], pair_recv.at[3], partner)
+    last_blocks(wa, 0)
+    weight_a = wa[...].reshape(depth, cut)
+    qs[:, :cut] = jnp.dot(theirs, weight_a, preferred_element_type=f32).astype(bf16)
+    send(qs.at[:, 0:cut], qr.at[:, 0:cut], pair_send.at[1], pair_recv.at[1], partner)
     pump(2)
     ours = xn[yl]
     got_a = jnp.dot(ours, weight_a, preferred_element_type=f32)
@@ -333,22 +336,23 @@
         )
         mixed = mixed + e0.astype(bf16).astype(f32) * v0 + e1.astype(bf16).astype(f32) * v1
         att3[part] = mixed / total
-    attended = jnp.concatenate(
-        [
-            jnp.concatenate([att3[:, s * heads + h, :] for h in range(heads)], axis=1)
-            for s in range(2)
-        ],
-        axis=0,
-    ).astype(bf16)
-    order = one_hot_rows(
-        (2, NZ, 2, NX), lambda r_, z_, s_, x_: s_ * rows + r_ * half + z_ * NX + x_
-    )
-    attb[yl] = pick(order, attended).astype(bf16)
-    send(attb.at[yl], attb.at[yl], pair_send.at[2], pair_recv.at[2], partner)
-
+        if (r0 + CHUNK) % half == 0:
+            lo = r0 + CHUNK - half
+            attended = jnp.concatenate(
+                [
+                    jnp.concatenate([att3[lo:lo + half, s * heads + h, :] for h in range(heads)], axis=1)
+                    for s in range(2)
+                ],
+                axis=0,
+            ).astype(bf16)
+            attb[yl, 2 * lo:2 * (lo + half), :] = pick(order, attended).astype(bf16)
+            group = attb.at[yl, pl.ds(2 * lo, rows)]
+            send(group, group, pair_send.at[4 + lo // half], pair_recv.at[4 + lo // half], partner)
     pump(len(out_steps))
-    stream_end(oa, ob, 1)
-    arrived(attb.at[1 - yl], pair_recv.at[2])
+    near = z // (NZ // 2)
+    wait_spread(ob, 1, near)
+    for r in range(2):
+        arrived(attb.at[1 - yl, pl.ds(r * rows, rows)], pair_recv.at[4 + r])
     full = attb[...].reshape(2 * both, heads * size)
     tiles = NYH // 2
     slab = NZ // tile_blocks
@@ -361,9 +365,6 @@
             full[:, :ocut], left, dims, preferred_element_type=f32
         ) + lax.dot_general(full[:, ocut:], right, dims, preferred_element_type=f32)
 
-    for i in range(tiles):
-        ps[i] = project(2 * i + 1 - c).astype(bf16)
-        send(ps.at[i], pr.at[i], core_send.at[i], core_recv.at[i], sib)
     def at(yy):
         yy = lax.rem(yy + ny, ny)
         return dev(x, z, lax.rem(yy, 2), yy // 2, c)
@@ -385,7 +386,13 @@
     def near_copy(m, h, side, to):
         return remote(sp.at[m, :, cuts[h]], rb.at[side, :, cuts[h]], y_send.at[m, h], y_recv.at[side, h], to)
 
-    for i in range(tiles):
+    half_tiles = (near, 1 - near)
+    for n, i in enumerate(half_tiles):
+        if n == 1:
+            last_blocks(oa, 1)
+            wait_spread(ob, 1, i)
+        ps[i] = project(2 * i + 1 - c).astype(bf16)
+        send(ps.at[i], pr.at[i], core_send.at[i], core_recv.at[i], sib)
         kept = project(2 * i + c)
         arrived(pr.at[i], core_recv.at[i])
         summed = (kept + pr[i].astype(f32)).astype(bf16)
@@ -404,7 +411,7 @@
                     pl.when(delta == 2)(near_copy(m, h, 0, at(NYH * yl + m)).start)
     for h in range(2):
         lanes = slice(0, split) if h == 0 else slice(split, width)
-        for m in range(NYH):
+        for m in [2 * i + r for i in half_tiles for r in range(2)]:
             delta = ahead(m)
 
             @pl.when(either(delta, 1, 7, 2 if h == 0 else 6))
@@ -459,7 +466,7 @@
     for s, buf in ((0, wb), (1, ob)):
         for d in range(1, NX):
             view = buf.at[:, mine]
-            remote(view, view, bx_send.at[s, d - 1], bx_recv.at[s, d - 1], sib).wait_send()
+            remote(view, view, bx_send.at[s, d - 1], bx_recv.at[s, d - 1, 0], sib).wait_send()
     for k in range(NYH):
         is_self = jnp.logical_and(yl_to == yl, yh == k)
         away = remote(xs, xg.at[yl, tile_me], xs_send.at[k], xs_recv.at[src_me], sib)
@@ -525,8 +532,8 @@
             dma(2),
             dma(NYH), dma(NYH), dma(NYH), dma(NYH), dma(2), dma(2),
             dma(2, NX - 1), dma(2, NX - 1), dma(2, 2, steps, NX), dma(2, 2, steps, NX),
-            dma(2, NX - 1), dma(2, NX - 1), dma(2, 2, steps), dma(2, 2, steps),
-            dma(4), dma(4), dma(NYH // 2), dma(NYH // 2), dma(NYH, 2), dma(NYH, 2), dma(2, 2),
+            dma(2, NX - 1), dma(2, NX - 1, 2), dma(2, 2, steps), dma(2, 2, steps),
+            dma(6), dma(6), dma(NYH // 2), dma(NYH // 2), dma(NYH, 2), dma(NYH, 2), dma(2, 2),
             dma(2, NZ - 1), dma(2, NZ - 1), dma(2, NX - 1), dma(2, NX - 1),
         ],
         compiler_params=pltpu.CompilerParams(

time: 99.7 us -> 97.3 us (0.976)
  Pallas kernels: 97.9 us -> 95.5 us
    pallas_call x1, Pallas kernels: 97.9 us -> 95.5 us  [on_device(): pl.pallas_call(layer_kernel, out_shape=jax.ShapeDtypeStruct((both, width)...]
where the time goes in v5:
time: 97.3 us; the launch traced here: 97.1 us
  Pallas kernels  95.5 us (98%)
  local copies, waits for them, and re-layouts  1.65 us (2%)
    pallas_call x1, Pallas kernels, on_device(): pl.pallas_call(layer_kernel, out_shape=jax.ShapeDtypeStruct((both, width)...  95.5 us

profile of v5, /device:TPU:1, one launch (start us, length us, event | category | flops | bytes accessed | tf_op | source)
XLA Modules:
  0.0 97.1 jit_solution(16031026755858535243)
XLA Ops:
  0.0 95.5 %gathered_layer.1 = bf16[128,640]{1,0:T(8,128)(2,1)} custom-call(bf16[64,640]{1,0:T(8,128)(2,1)} %hid.1, bf16[64,640]{1,0:T(8,128)(2,1)} %nxt.1, bf16[40,128]{1,0:T(8,128)(2,1)} %bitcast.10, bf16[80,512]{1,0:T(8,128)(2,1)} %wq.1, bf16[80,128]{1,0:T(8,128)(2,1)} %wk.1, bf16[80,128]{1,0:T(8,128)(2,1)} %wv.1, bf16[80,512]{1,0:T(8,128)(2,1)} %bitcast.9, ...), custom_call_target="tpu_custom_call" | custom-call | tf_op jit(solution)/shard_map/gathered_layer/pallas_call | solution.py:499
  95.5 1.6 %reshape.15 = bf16[64,2,1,640]{3,1,0,2:T(2,128)(2,1)} reshape(bf16[128,640]{1,0:T(8,128)(2,1)} %gathered_layer.1) | data formatting | bytes 327680 | tf_op jit(solution)/shard_map/reshape | solution.py:548

commit v6 on v5

--- a/solution.py
+++ b/solution.py
@@ -37,9 +37,9 @@
 
 
 def layer_kernel(
-    hid, nxt, gain, wq, wk, wv, wot, freq_ref, len_ref, pos_ref, kc_hbm, vc_hbm,
+    hid, nxt, gain, wq, wk, wv, wot, freq_hbm, len_hbm, pos_hbm, kc_hbm, vc_hbm,
     out,
-    wa, wb, oa, ob, xs, xg, xn, wide, ssb, ssr, qs, qr, kc, vc, q3, att3, attb,
+    freq_ref, len_ref, pos_ref, load_sem, wa, wb, oa, ob, xs, xg, xn, wide, ssb, ssr, qs, qr, kc, vc, q3, att3, attb,
     ps, pr, sp, fb, rb, rr, zs, zr, xo, xr,
     cache_sem, xs_send, xs_recv, sib_send, sib_recv, res_send, res_recv,
     ax_send, ax_recv, az_send, az_recv, bx_send, bx_recv, bz_send, bz_recv,
@@ -76,10 +76,23 @@
         copy.start()
         sent.append(copy)
 
-    key_load = pltpu.make_async_copy(kc_hbm, kc, cache_sem.at[0])
-    value_load = pltpu.make_async_copy(vc_hbm, vc, cache_sem.at[1])
-    key_load.start()
-    value_load.start()
+    mine = pl.ds(pl.multiple_of(x * block, block), block)
+    cut, ocut = wa.shape[2], oa.shape[2]
+    qcols, size = wq.shape[1], kc.shape[2]
+    loads = [
+        (hid, xs.at[pl.ds(0, rows)]),
+        (nxt, xs.at[pl.ds(rows, rows)]),
+        (wq.at[:, pl.ds(0, cut)], wa.at[z, mine]),
+        (wq.at[:, pl.ds(cut, qcols - cut)], wb.at[z, mine, pl.ds(0, qcols - cut)]),
+        (wk, wb.at[z, mine, pl.ds(qcols - cut, size)]),
+        (wv, wb.at[z, mine, pl.ds(qcols - cut + size, size)]),
+        (wot.at[:, pl.ds(0, ocut)], oa.at[z, mine]),
+        (wot.at[:, pl.ds(ocut, qcols - ocut)], ob.at[z, mine]),
+        (freq_hbm, freq_ref), (len_hbm, len_ref), (pos_hbm, pos_ref),
+    ]
+    loads = [pltpu.make_async_copy(src, dst, load_sem.at[n]) for n, (src, dst) in enumerate(loads)]
+    for load in loads:
+        load.start()
 
     y = 2 * yh + yl
     ny = 2 * NYH
@@ -95,17 +108,11 @@
     for where in places:
         pl.semaphore_signal(barrier, inc=1, device_id=where, device_id_type=MESH)
 
-    mine = pl.ds(pl.multiple_of(x * block, block), block)
-    cut = wa.shape[2]
-    own = jnp.concatenate([wq[...], wk[...], wv[...]], axis=1)
-    wa[z, mine, :] = own[:, :cut]
-    wb[z, mine, :] = own[:, cut:]
-    ocut = oa.shape[2]
-    oa[z, mine, :] = wot[:, :ocut]
-    ob[z, mine, :] = wot[:, ocut:]
-    xs[0:rows, :] = hid[...]
-    xs[rows:both, :] = nxt[...]
+    for load in loads:
+        load.wait()
     pl.semaphore_wait(barrier, len(places))
+    key_load = pltpu.make_async_copy(kc_hbm, kc, cache_sem.at[0])
+    value_load = pltpu.make_async_copy(vc_hbm, vc, cache_sem.at[1])
 
     yl_to = yh // (NYH // 2)
     tile_me = lax.rem(yh, NYH // 2) * 2 + c
@@ -193,6 +200,15 @@
             a_wait(a_buf, s, k, i)
             a_send(a_buf, s, k + 1, i)
 
+        if s == 1:
+            firsts = [functools.partial(from_x, i) for i in range(1, NX)]
+            smalls = [functools.partial(b_step, k) for k in range(last + 1)]
+            larges = [functools.partial(a_step, k, i) for k in range(last) for i in range(NX)]
+            steps = [start] + firsts[:1] + smalls[:1] + firsts[1:]
+            for small in smalls[1:]:
+                steps += larges[:2] + [small]
+                larges = larges[2:]
+            return steps + larges
         steps = [start]
         steps += [functools.partial(from_x, i) for i in range(1, NX)]
         for k in range(last + 1):
@@ -228,14 +244,16 @@
         return jnp.sum(jnp.where(diagonal, spread, 0.0), axis=1, keepdims=True)
 
     size = kc.shape[2]
-    for step in in_steps:
+    for number, step in enumerate(in_steps):
         step()
+        if number == 2 * len(in_steps) // 3:
+            pump(1)
 
     for k in range(NYH):
         slot = xg.at[k // (NYH // 2), (k % (NYH // 2)) * 2 + c]
         arrived(slot, xs_recv.at[k])
         send(slot, slot, sib_send.at[k], sib_recv.at[k], sib)
-    pump(1)
+    pump(3)
     for k in range(NYH):
         arrived(xg.at[k // (NYH // 2), (k % (NYH // 2)) * 2 + (1 - c)], sib_recv.at[k])
 
@@ -255,6 +273,8 @@
     send(ssb.at[1 - yl], ssr, pair_send.at[0], pair_recv.at[0], partner)
     pump(2)
 
+    key_load.start()
+    value_load.start()
     first_at = as_column(pos_ref)
     angle = jnp.concatenate([first_at, first_at + 1.0], axis=0) * freq_ref[...]
     lane = lax.broadcasted_iota(jnp.int32, (both, size), 1)
@@ -268,7 +288,7 @@
     for g in range(2):
         rr[g] = pick(order, rr[g]).astype(bf16)
 
-    pump(1)
+    pump(2)
     wait_spread(wb, 0, 0)
     wait_spread(wb, 0, 1)
     depth = NZ * NX * block
@@ -292,9 +312,9 @@
     inverse = lax.rsqrt(square[:, :1] + RMS_EPS)
     arrived(qr.at[:, 0:cut], pair_recv.at[1])
     arrived(qr.at[:, rest], pair_recv.at[3])
-    pump(1)
+    pump(2)
     got = (got + qr[...].astype(f32)) * inverse
-    heads = wq.shape[1] // size
+    heads = qcols // size
 
     def rotated(v):
         return (v * cosine + pltpu.roll(v, size // 2, 1) * sine).astype(bf16).astype(f32)
@@ -499,9 +519,13 @@
     result = pl.pallas_call(
         layer_kernel,
         out_shape=jax.ShapeDtypeStruct((both, width), bf16),
-        in_specs=[vmem] * 10 + [hbm] * 2,
+        in_specs=[hbm] * 2 + [vmem] + [hbm] * 9,
         out_specs=vmem,
         scratch_shapes=[
+            pltpu.VMEM((1, size), f32),
+            pltpu.VMEM((1, rows), jnp.int32),
+            pltpu.VMEM((1, rows), jnp.int32),
+            dma(11),
             pltpu.VMEM((NZ, NX * block, cut), bf16),
             pltpu.VMEM((NZ, NX * block, columns - cut), bf16),
             pltpu.VMEM((NZ, NX * block, ocut), bf16),

time: 97.3 us -> 98.9 us (1.016)
  Pallas kernels: 95.5 us -> 97.1 us
    pallas_call x1, Pallas kernels: 95.5 us -> 97.1 us  [on_device(): pl.pallas_call(layer_kernel, out_shape=jax.ShapeDtypeStruct((both, width)...]
where the time goes in v6:
time: 98.9 us; the launch traced here: 98.7 us
  Pallas kernels  97.1 us (98%)
  local copies, waits for them, and re-layouts  1.65 us (2%)
    pallas_call x1, Pallas kernels, on_device(): pl.pallas_call(layer_kernel, out_shape=jax.ShapeDtypeStruct((both, width)...  97.1 us

profile of v6, /device:TPU:1, one launch (start us, length us, event | category | flops | bytes accessed | tf_op | source)
XLA Modules:
  0.0 98.7 jit_solution(14562844871560135396)
XLA Ops:
  0.0 97.1 %gathered_layer.1 = bf16[128,640]{1,0:T(8,128)(2,1)} custom-call(bf16[64,640]{1,0:T(8,128)(2,1)} %hid.1, bf16[64,640]{1,0:T(8,128)(2,1)} %nxt.1, bf16[40,128]{1,0:T(8,128)(2,1)} %bitcast.10, bf16[80,512]{1,0:T(8,128)(2,1)} %wq.1, bf16[80,128]{1,0:T(8,128)(2,1)} %wk.1, bf16[80,128]{1,0:T(8,128)(2,1)} %wv.1, bf16[80,512]{1,0:T(8,128)(2,1)} %bitcast.9, ...), custom_call_target="tpu_custom_call" | custom-call | tf_op jit(solution)/shard_map/gathered_layer/pallas_call | solution.py:519
  97.1 1.6 %reshape.15 = bf16[64,2,1,640]{3,1,0,2:T(2,128)(2,1)} reshape(bf16[128,640]{1,0:T(8,128)(2,1)} %gathered_layer.1) | data formatting | bytes 327680 | tf_op jit(solution)/shard_map/reshape | solution.py:572

commit v7 on v5

--- a/solution.py
+++ b/solution.py
@@ -228,14 +228,15 @@
         return jnp.sum(jnp.where(diagonal, spread, 0.0), axis=1, keepdims=True)
 
     size = kc.shape[2]
-    for step in in_steps:
+    for number, step in enumerate(in_steps):
         step()
+        if number == 1 * len(in_steps) // 2:
+            pump(1)
 
     for k in range(NYH):
         slot = xg.at[k // (NYH // 2), (k % (NYH // 2)) * 2 + c]
         arrived(slot, xs_recv.at[k])
         send(slot, slot, sib_send.at[k], sib_recv.at[k], sib)
-    pump(1)
     for k in range(NYH):
         arrived(xg.at[k // (NYH // 2), (k % (NYH // 2)) * 2 + (1 - c)], sib_recv.at[k])
 

time: 97.3 us -> 98.4 us (1.011)
  Pallas kernels: 95.5 us -> 96.6 us
    pallas_call x1, Pallas kernels: 95.5 us -> 96.6 us  [on_device(): pl.pallas_call(layer_kernel, out_shape=jax.ShapeDtypeStruct((both, width)...]
where the time goes in v7:
time: 98.4 us; the launch traced here: 98.2 us
  Pallas kernels  96.6 us (98%)
  local copies, waits for them, and re-layouts  1.65 us (2%)
    pallas_call x1, Pallas kernels, on_device(): pl.pallas_call(layer_kernel, out_shape=jax.ShapeDtypeStruct((both, width)...  96.6 us

profile of v7, /device:TPU:1, one launch (start us, length us, event | category | flops | bytes accessed | tf_op | source)
XLA Modules:
  0.0 98.2 jit_solution(6222753274794473385)
XLA Ops:
  0.0 96.6 %gathered_layer.1 = bf16[128,640]{1,0:T(8,128)(2,1)} custom-call(bf16[64,640]{1,0:T(8,128)(2,1)} %hid.1, bf16[64,640]{1,0:T(8,128)(2,1)} %nxt.1, bf16[40,128]{1,0:T(8,128)(2,1)} %bitcast.10, bf16[80,512]{1,0:T(8,128)(2,1)} %wq.1, bf16[80,128]{1,0:T(8,128)(2,1)} %wk.1, bf16[80,128]{1,0:T(8,128)(2,1)} %wv.1, bf16[80,512]{1,0:T(8,128)(2,1)} %bitcast.9, ...), custom_call_target="tpu_custom_call" | custom-call | tf_op jit(solution)/shard_map/gathered_layer/pallas_call | solution.py:500
  96.6 1.6 %reshape.15 = bf16[64,2,1,640]{3,1,0,2:T(2,128)(2,1)} reshape(bf16[128,640]{1,0:T(8,128)(2,1)} %gathered_layer.1) | data formatting | bytes 327680 | tf_op jit(solution)/shard_map/reshape | solution.py:549
